TPU v7x, 32 devices: a whole 2x2x4 slice. The times are simulated.
32 devices in a mesh: ctx: 8 (over z, x), fsdp: 4 (over y, core).
Axes of the slice: x: 2, y: 2, z: 4, core: 2. Of those that a mesh axis runs over, the one named last changes fastest.
Arguments:
- hidden_in: bfloat16 [4, 1024, 1536], P('fsdp', 'ctx'), may hold values from -6 to 6
- cotangent: bfloat16 [4, 1024, 1536], P('fsdp', 'ctx'), may hold values from -6 to 6
- block_order: int32 [4, 16], P('fsdp'), may hold values from 0 to 15, as said below
- rotary_positions: int32 [4, 1024], P('fsdp', 'ctx'), may hold values from 0 to 2046, as said below
- attn_gain: bfloat16 [1536], P(('ctx', 'fsdp')), may hold values from 0.25 to 1.75
- qk_gain: bfloat16 [128], P(('ctx', 'fsdp')), may hold values from 0.25 to 1.75
- w_query: bfloat16 [1536, 1536], P(('ctx', 'fsdp')), may hold values from -0.15625 to 0.15625
- key_projection: bfloat16 [1536, 512], P(('ctx', 'fsdp')), may hold values from -0.15625 to 0.15625
- value_projection: bfloat16 [1536, 512], P(('ctx', 'fsdp')), may hold values from -0.15625 to 0.15625
- w_output: bfloat16 [1536, 1536], P(('ctx', 'fsdp')), may hold values from -1 to 1
- ffn_gain: bfloat16 [1536], P(('ctx', 'fsdp')), may hold values from 0.25 to 1.75
- w_gate: bfloat16 [1536, 4608], P(('ctx', 'fsdp')), may hold values from -0.15625 to 0.15625
- w_up: bfloat16 [1536, 4608], P(('ctx', 'fsdp')), may hold values from -0.15625 to 0.15625
- w_down: bfloat16 [4608, 1536], P(('ctx', 'fsdp')), may hold values from -0.09375 to 0.09375
Outputs:
- block_out: bfloat16 [4, 1024, 1536], P('fsdp', 'ctx')
- grad_in: bfloat16 [4, 1024, 1536], P('fsdp', 'ctx')
- grad_attn_gain: float32 [1536], P(('ctx', 'fsdp'))
- grad_qk_gain: float32 [128], P(('ctx', 'fsdp'))
- grad_w_query: float32 [1536, 1536], P(('ctx', 'fsdp'))
- grad_w_key: float32 [1536, 512], P(('ctx', 'fsdp'))
- grad_w_value: float32 [1536, 512], P(('ctx', 'fsdp'))
- grad_w_output: float32 [1536, 1536], P(('ctx', 'fsdp'))
- grad_ffn_gain: float32 [1536], P(('ctx', 'fsdp'))
- grad_w_gate: float32 [1536, 4608], P(('ctx', 'fsdp'))
- grad_w_up: float32 [1536, 4608], P(('ctx', 'fsdp'))
- grad_w_down: float32 [4608, 1536], P(('ctx', 'fsdp'))
Inputs may be any that keep to these rules, and one draw needn't show every extreme that they name: Row s is an ordering of the 16 blocks of 64 consecutive tokens of sequence s: stored slot j holds block block_order[s, j], so device i of ctx holds slots 2 i and 2 i + 1. `rotary_positions`: A token's rotary position is its place in its sequence (seq_index) plus one start per sequence, the start from 0 to 1023; the first sequence starts at 0 and the last at 1023.
All inputs are finite; a program needn't handle non-finite values.
Results may differ from a plain program's by a relative error of at most 0.019.
Values may be sent and summed in bfloat16 or wider, within the bound.
A program may use at most 384 MiB of HBM per device.

v0:
```python
import math

import jax
import jax.numpy as jnp
from jax import lax
from jax.sharding import PartitionSpec as P

QUERY_HEADS = 24
KEY_VALUE_HEADS = 8
HEAD_SIZE = 64


EPS = 1e-05
THETA = 1000000.0


def frequencies(model_width):
    return jnp.exp(
        -math.log(THETA) * 2.0 * jnp.arange(model_width // 2, dtype=jnp.float32) / model_width
    )


def apply_rotary(value_matrix_rows, rotary_angles):
    half = value_matrix_rows.shape[-1] // 2
    cosine = jnp.cos(rotary_angles)[:, None, :]
    sine = jnp.sin(rotary_angles)[:, None, :]
    first = value_matrix_rows[..., :half]
    second = value_matrix_rows[..., half:]
    return jnp.concatenate(
        [first * cosine - second * sine, second * cosine + first * sine], axis=-1
    )


def rotary_backward(grads, rotary_angles):
    half = grads.shape[-1] // 2
    cosine = jnp.cos(rotary_angles)[:, None, :]
    sine = jnp.sin(rotary_angles)[:, None, :]
    first = grads[..., :half]
    second = grads[..., half:]
    return jnp.concatenate(
        [first * cosine + second * sine, second * cosine - first * sine], axis=-1
    )


def norm_backward(value_matrix_rows, inverse, gain, grads):
    weighted = grads * gain
    return inverse * weighted - inverse * inverse * inverse * value_matrix_rows * jnp.mean(
        weighted * value_matrix_rows, axis=-1, keepdims=True
    )


def lookup(table, slots):
    matches = slots[:, None] == jnp.arange(table.shape[0], dtype=jnp.int32)[None, :]
    return jnp.sum(jnp.where(matches, table[None, :], 0), axis=1)


def sequence_index(table, places, half_rows):
    return lookup(table, places // half_rows) * half_rows + places % half_rows


def block_scores(grouped_heads, key_rows):
    model_width = key_rows.shape[0]
    reshaped_heads = key_rows.reshape(model_width, KEY_VALUE_HEADS, HEAD_SIZE)
    return jnp.einsum(
        "thgd,khd->hgtk", grouped_heads, reshaped_heads, preferred_element_type=jnp.float32
    ) * (1.0 / math.sqrt(HEAD_SIZE))


def owner_totals(received):
    return tuple((jnp.sum(piece, axis=0) for piece in received))


def sweep(state, pieces, start, step, table, half_rows, last_query):
    token_count = pieces[0].shape[0]
    model_width = max(
        (size for size in range(1, min(token_count, 512) + 1) if token_count % size == 0)
    )
    turns = token_count // model_width
    stacked = tuple((piece.reshape((turns, model_width) + piece.shape[1:]) for piece in pieces))
    offsets = start + model_width * jnp.arange(turns, dtype=jnp.int32)

    def visit(carry, item):
        parts, position_shift = item
        key_index = sequence_index(
            table, position_shift + jnp.arange(model_width, dtype=jnp.int32), half_rows
        )
        live = jnp.min(key_index) <= last_query
        carry = lax.cond(
            live,
            lambda inner: step(inner, parts, position_shift, key_index),
            lambda inner: inner,
            carry,
        )
        return (carry, None)

    state, unused = lax.scan(visit, state, (stacked, offsets))
    return state


def on_device(
    hidden_in,
    cotangent,
    block_order,
    rotary_positions,
    attn_gain,
    qk_gain,
    w_query,
    key_projection,
    value_projection,
    w_output,
    ffn_gain,
    w_gate,
    w_up,
    w_down,
):
    single_float = jnp.float32
    brain_float_half = jnp.bfloat16
    gathered = (
        lax.all_gather(attn_gain, ("ctx", "fsdp"), axis=0, tiled=True),
        lax.all_gather(qk_gain, ("ctx", "fsdp"), axis=0, tiled=True),
        lax.all_gather(w_query, ("ctx", "fsdp"), axis=0, tiled=True),
        lax.all_gather(key_projection, ("ctx", "fsdp"), axis=0, tiled=True),
        lax.all_gather(value_projection, ("ctx", "fsdp"), axis=0, tiled=True),
        lax.all_gather(w_output, ("ctx", "fsdp"), axis=0, tiled=True),
        lax.all_gather(ffn_gain, ("ctx", "fsdp"), axis=0, tiled=True),
        lax.all_gather(w_gate, ("ctx", "fsdp"), axis=0, tiled=True),
        lax.all_gather(w_up, ("ctx", "fsdp"), axis=0, tiled=True),
        lax.all_gather(w_down, ("ctx", "fsdp"), axis=0, tiled=True),
    )
    gain_one, gain_both, query_w, key_matrix, value_w, output_w, gain_two, gate_w, up_w, down_w = (
        gathered
    )
    gain_one = gain_one.astype(single_float)
    gain_two = gain_two.astype(single_float)
    gain_query = gain_both[:HEAD_SIZE].astype(single_float)
    key_norm_gain = gain_both[HEAD_SIZE:].astype(single_float)
    queries_per_group = QUERY_HEADS // KEY_VALUE_HEADS
    hidden = hidden_in[0].astype(single_float)
    grad_out = cotangent[0]
    token_rows = hidden.shape[0]
    half_rows = token_rows // 2
    sequence_span = token_rows * lax.axis_size("ctx")
    order = block_order[0]
    place = lax.axis_index("ctx")
    local_rows = jnp.arange(token_rows, dtype=jnp.int32)
    my_index = sequence_index(order, place * token_rows + local_rows, half_rows)
    last_query = jnp.max(my_index)
    rotary_angles = (
        rotary_positions[0].astype(single_float)[:, None] * frequencies(HEAD_SIZE)[None, :]
    )
    inv_one = lax.rsqrt(jnp.mean(hidden * hidden, axis=-1, keepdims=True) + EPS)
    normalized_input = (hidden * inv_one * gain_one).astype(brain_float_half)
    query_rows = jnp.dot(normalized_input, query_w, preferred_element_type=single_float).reshape(
        token_rows, QUERY_HEADS, HEAD_SIZE
    )
    key = jnp.dot(normalized_input, key_matrix, preferred_element_type=single_float).reshape(
        token_rows, KEY_VALUE_HEADS, HEAD_SIZE
    )
    value_rows = jnp.dot(normalized_input, value_w, preferred_element_type=single_float).astype(
        brain_float_half
    )
    inv_query = lax.rsqrt(jnp.mean(query_rows * query_rows, axis=-1, keepdims=True) + EPS)
    key_inverse_norm = lax.rsqrt(jnp.mean(key * key, axis=-1, keepdims=True) + EPS)
    rotated_query = apply_rotary(query_rows * inv_query * gain_query, rotary_angles).astype(
        brain_float_half
    )
    rotated_key = (
        apply_rotary(key * key_inverse_norm * key_norm_gain, rotary_angles)
        .astype(brain_float_half)
        .reshape(token_rows, KEY_VALUE_HEADS * HEAD_SIZE)
    )
    grouped_heads = rotated_query.reshape(token_rows, KEY_VALUE_HEADS, queries_per_group, HEAD_SIZE)

    def allowed_of(key_index):
        return (key_index[None, :] <= my_index[:, None])[None, None]

    def stats_step(carry, parts, position_shift, key_index):
        running, total = carry
        scores = jnp.where(allowed_of(key_index), block_scores(grouped_heads, parts[0]), -jnp.inf)
        newer = jnp.maximum(running, jnp.max(scores, axis=-1))
        total = total * jnp.exp(running - newer) + jnp.sum(
            jnp.exp(scores - newer[..., None]), axis=-1
        )
        return (newer, total)

    statistic_shape = (KEY_VALUE_HEADS, queries_per_group, token_rows)
    running, total = sweep(
        (jnp.full(statistic_shape, -1e30, single_float), jnp.zeros(statistic_shape, single_float)),
        (lax.all_gather(rotated_key, "ctx", axis=0, tiled=True),),
        jnp.int32(0),
        stats_step,
        order,
        half_rows,
        last_query,
    )
    log_total = running + jnp.log(total)

    def probs_of(key_rows, key_index):
        return jnp.where(
            allowed_of(key_index),
            jnp.exp(block_scores(grouped_heads, key_rows) - log_total[..., None]),
            0.0,
        )

    def mix_step(carry, parts, position_shift, key_index):
        key_rows, value_matrix_rows = parts
        probs_low = probs_of(key_rows, key_index).astype(brain_float_half)
        reshaped_heads = value_matrix_rows.reshape(key_rows.shape[0], KEY_VALUE_HEADS, HEAD_SIZE)
        return carry + jnp.einsum(
            "hgtk,khd->thgd", probs_low, reshaped_heads, preferred_element_type=single_float
        )

    mixed_sum = sweep(
        jnp.zeros((token_rows, KEY_VALUE_HEADS, queries_per_group, HEAD_SIZE), single_float),
        (
            lax.all_gather(rotated_key, "ctx", axis=0, tiled=True),
            lax.all_gather(value_rows, "ctx", axis=0, tiled=True),
        ),
        jnp.int32(0),
        mix_step,
        order,
        half_rows,
        last_query,
    )
    mixed = mixed_sum.reshape(token_rows, QUERY_HEADS * HEAD_SIZE).astype(brain_float_half)
    middle = hidden + jnp.dot(mixed, output_w, preferred_element_type=single_float)
    inv_two = lax.rsqrt(jnp.mean(middle * middle, axis=-1, keepdims=True) + EPS)
    normed_two = (middle * inv_two * gain_two).astype(brain_float_half)
    gate = jnp.dot(normed_two, gate_w, preferred_element_type=single_float)
    up = jnp.dot(normed_two, up_w, preferred_element_type=single_float)
    sigmoid_gate = jax.nn.sigmoid(gate)
    active = gate * sigmoid_gate
    inner = (active * up).astype(brain_float_half)
    block_out = (middle + jnp.dot(inner, down_w, preferred_element_type=single_float)).astype(
        brain_float_half
    )
    regathered = (
        lax.all_gather(attn_gain, ("ctx", "fsdp"), axis=0, tiled=True),
        lax.all_gather(qk_gain, ("ctx", "fsdp"), axis=0, tiled=True),
        lax.all_gather(w_query, ("ctx", "fsdp"), axis=0, tiled=True),
        lax.all_gather(key_projection, ("ctx", "fsdp"), axis=0, tiled=True),
        lax.all_gather(value_projection, ("ctx", "fsdp"), axis=0, tiled=True),
        lax.all_gather(w_output, ("ctx", "fsdp"), axis=0, tiled=True),
        lax.all_gather(ffn_gain, ("ctx", "fsdp"), axis=0, tiled=True),
        lax.all_gather(w_gate, ("ctx", "fsdp"), axis=0, tiled=True),
        lax.all_gather(w_up, ("ctx", "fsdp"), axis=0, tiled=True),
        lax.all_gather(w_down, ("ctx", "fsdp"), axis=0, tiled=True),
    )
    (
        unused_one,
        unused_both,
        query_w,
        key_matrix,
        value_w,
        output_w,
        unused_two,
        gate_w,
        up_w,
        down_w,
    ) = regathered
    grad_w_down = jnp.einsum("tf,td->fd", inner, grad_out, preferred_element_type=single_float)
    grad_inner = jnp.einsum("td,fd->tf", grad_out, down_w, preferred_element_type=single_float)
    grad_gate = (grad_inner * up * sigmoid_gate * (1.0 + gate * (1.0 - sigmoid_gate))).astype(
        brain_float_half
    )
    grad_up = (grad_inner * active).astype(brain_float_half)
    grad_w_gate = jnp.einsum(
        "td,tf->df", normed_two, grad_gate, preferred_element_type=single_float
    )
    grad_w_up = jnp.einsum("td,tf->df", normed_two, grad_up, preferred_element_type=single_float)
    grad_normed_two = jnp.einsum(
        "tf,df->td", grad_gate, gate_w, preferred_element_type=single_float
    ) + jnp.einsum("tf,df->td", grad_up, up_w, preferred_element_type=single_float)
    grad_ffn_gain = jnp.sum(grad_normed_two * middle * inv_two, axis=0)
    grad_middle = grad_out.astype(single_float) + norm_backward(
        middle, inv_two, gain_two, grad_normed_two
    )
    grad_branch = grad_middle.astype(brain_float_half)
    grad_w_output = jnp.einsum("tq,td->qd", mixed, grad_branch, preferred_element_type=single_float)
    mixed_gradient = jnp.einsum(
        "td,qd->tq", grad_branch, output_w, preferred_element_type=single_float
    ).astype(brain_float_half)
    gradient_of_grouped = mixed_gradient.reshape(
        token_rows, KEY_VALUE_HEADS, queries_per_group, HEAD_SIZE
    )
    delta = jnp.transpose(
        jnp.sum(gradient_of_grouped.astype(single_float) * mixed_sum, axis=-1), (1, 2, 0)
    )

    def back_step(carry, parts, position_shift, key_index):
        grad_query_acc, key_gradient_total, value_gradient_total = carry
        key_rows, value_matrix_rows = parts
        model_width = key_rows.shape[0]
        probs = probs_of(key_rows, key_index)
        probs_low = probs.astype(brain_float_half)
        reshaped_keys = key_rows.reshape(model_width, KEY_VALUE_HEADS, HEAD_SIZE)
        reshaped_values = value_matrix_rows.reshape(model_width, KEY_VALUE_HEADS, HEAD_SIZE)
        grad_probs = jnp.einsum(
            "thgd,khd->hgtk",
            gradient_of_grouped,
            reshaped_values,
            preferred_element_type=single_float,
        )
        grad_scores = (probs * (grad_probs - delta[..., None])).astype(brain_float_half)
        grad_query_acc = grad_query_acc + jnp.einsum(
            "hgtk,khd->thgd", grad_scores, reshaped_keys, preferred_element_type=single_float
        )
        keys_gradient = jnp.einsum(
            "hgtk,thgd->khd", grad_scores, grouped_heads, preferred_element_type=single_float
        ) * (1.0 / math.sqrt(HEAD_SIZE))
        values_gradient = jnp.einsum(
            "hgtk,thgd->khd", probs_low, gradient_of_grouped, preferred_element_type=single_float
        )
        key_gradient_total = lax.dynamic_update_slice_in_dim(
            key_gradient_total,
            keys_gradient.reshape(model_width, KEY_VALUE_HEADS * HEAD_SIZE),
            position_shift,
            0,
        )
        value_gradient_total = lax.dynamic_update_slice_in_dim(
            value_gradient_total,
            values_gradient.reshape(model_width, KEY_VALUE_HEADS * HEAD_SIZE),
            position_shift,
            0,
        )
        return (grad_query_acc, key_gradient_total, value_gradient_total)

    zero_gradients = jnp.zeros((sequence_span, KEY_VALUE_HEADS * HEAD_SIZE), single_float)
    grad_query_acc, key_gradient_total, value_gradient_total = sweep(
        (
            jnp.zeros((token_rows, KEY_VALUE_HEADS, queries_per_group, HEAD_SIZE), single_float),
            zero_gradients,
            zero_gradients,
        ),
        (
            lax.all_gather(rotated_key, "ctx", axis=0, tiled=True),
            lax.all_gather(value_rows, "ctx", axis=0, tiled=True),
        ),
        jnp.int32(0),
        back_step,
        order,
        half_rows,
        last_query,
    )
    key_gradient_local, grad_value_own = (
        lax.psum_scatter(
            key_gradient_total.astype(jnp.bfloat16), "ctx", scatter_dimension=0, tiled=True
        ).astype(jnp.float32),
        lax.psum_scatter(
            value_gradient_total.astype(jnp.bfloat16), "ctx", scatter_dimension=0, tiled=True
        ).astype(jnp.float32),
    )
    grad_query_rot = grad_query_acc.reshape(token_rows, QUERY_HEADS, HEAD_SIZE) * (
        1.0 / math.sqrt(HEAD_SIZE)
    )
    grad_query_norm = rotary_backward(grad_query_rot, rotary_angles)
    key_norm_gradient = rotary_backward(
        key_gradient_local.reshape(token_rows, KEY_VALUE_HEADS, HEAD_SIZE), rotary_angles
    )
    grad_gain_query = jnp.sum(grad_query_norm * query_rows * inv_query, axis=(0, 1))
    grad_gain_key = jnp.sum(key_norm_gradient * key * key_inverse_norm, axis=(0, 1))
    grad_qk_gain = jnp.concatenate([grad_gain_query, grad_gain_key], axis=0)
    grad_query = (
        norm_backward(query_rows, inv_query, gain_query, grad_query_norm)
        .reshape(token_rows, QUERY_HEADS * HEAD_SIZE)
        .astype(brain_float_half)
    )
    key_gradient = (
        norm_backward(key, key_inverse_norm, key_norm_gain, key_norm_gradient)
        .reshape(token_rows, KEY_VALUE_HEADS * HEAD_SIZE)
        .astype(brain_float_half)
    )
    grad_value = grad_value_own.astype(brain_float_half)
    grad_w_query = jnp.einsum(
        "td,tq->dq", normalized_input, grad_query, preferred_element_type=single_float
    )
    grad_w_key = jnp.einsum(
        "td,tq->dq", normalized_input, key_gradient, preferred_element_type=single_float
    )
    grad_w_value = jnp.einsum(
        "td,tq->dq", normalized_input, grad_value, preferred_element_type=single_float
    )
    grad_normed = jnp.einsum("tq,dq->td", grad_query, query_w, preferred_element_type=single_float)
    grad_normed = grad_normed + jnp.einsum(
        "tq,dq->td", key_gradient, key_matrix, preferred_element_type=single_float
    )
    grad_normed = grad_normed + jnp.einsum(
        "tq,dq->td", grad_value, value_w, preferred_element_type=single_float
    )
    grad_attn_gain = jnp.sum(grad_normed * hidden * inv_one, axis=0)
    grad_in = (grad_middle + norm_backward(hidden, inv_one, gain_one, grad_normed)).astype(
        brain_float_half
    )
    received = (
        lax.all_to_all(
            grad_attn_gain[None].astype(jnp.bfloat16),
            ("ctx", "fsdp"),
            split_axis=1,
            concat_axis=0,
            tiled=True,
        ).astype(jnp.float32),
        lax.all_to_all(
            grad_qk_gain[None].astype(jnp.bfloat16),
            ("ctx", "fsdp"),
            split_axis=1,
            concat_axis=0,
            tiled=True,
        ).astype(jnp.float32),
        lax.all_to_all(
            grad_w_query[None].astype(jnp.bfloat16),
            ("ctx", "fsdp"),
            split_axis=1,
            concat_axis=0,
            tiled=True,
        ).astype(jnp.float32),
        lax.all_to_all(
            grad_w_key[None].astype(jnp.bfloat16),
            ("ctx", "fsdp"),
            split_axis=1,
            concat_axis=0,
            tiled=True,
        ).astype(jnp.float32),
        lax.all_to_all(
            grad_w_value[None].astype(jnp.bfloat16),
            ("ctx", "fsdp"),
            split_axis=1,
            concat_axis=0,
            tiled=True,
        ).astype(jnp.float32),
        lax.all_to_all(
            grad_w_output[None].astype(jnp.bfloat16),
            ("ctx", "fsdp"),
            split_axis=1,
            concat_axis=0,
            tiled=True,
        ).astype(jnp.float32),
        lax.all_to_all(
            grad_ffn_gain[None].astype(jnp.bfloat16),
            ("ctx", "fsdp"),
            split_axis=1,
            concat_axis=0,
            tiled=True,
        ).astype(jnp.float32),
        lax.all_to_all(
            grad_w_gate[None].astype(jnp.bfloat16),
            ("ctx", "fsdp"),
            split_axis=1,
            concat_axis=0,
            tiled=True,
        ).astype(jnp.float32),
        lax.all_to_all(
            grad_w_up[None].astype(jnp.bfloat16),
            ("ctx", "fsdp"),
            split_axis=1,
            concat_axis=0,
            tiled=True,
        ).astype(jnp.float32),
        lax.all_to_all(
            grad_w_down[None].astype(jnp.bfloat16),
            ("ctx", "fsdp"),
            split_axis=1,
            concat_axis=0,
            tiled=True,
        ).astype(jnp.float32),
    )
    summed = owner_totals(received)
    return (
        block_out[None],
        grad_in[None],
        summed[0],
        summed[1],
        summed[2],
        summed[3],
        summed[4],
        summed[5],
        summed[6],
        summed[7],
        summed[8],
        summed[9],
    )


def solution(mesh):
    return jax.shard_map(
        on_device,
        mesh=mesh,
        in_specs=(
            P("fsdp", "ctx", None),
            P("fsdp", "ctx", None),
            P("fsdp", None),
            P("fsdp", "ctx"),
            P(("ctx", "fsdp")),
            P(("ctx", "fsdp")),
            P(("ctx", "fsdp"), None),
            P(("ctx", "fsdp"), None),
            P(("ctx", "fsdp"), None),
            P(("ctx", "fsdp"), None),
            P(("ctx", "fsdp")),
            P(("ctx", "fsdp"), None),
            P(("ctx", "fsdp"), None),
            P(("ctx", "fsdp"), None),
        ),
        out_specs=(
            P("fsdp", "ctx", None),
            P("fsdp", "ctx", None),
            P(("ctx", "fsdp")),
            P(("ctx", "fsdp")),
            P(("ctx", "fsdp"), None),
            P(("ctx", "fsdp"), None),
            P(("ctx", "fsdp"), None),
            P(("ctx", "fsdp"), None),
            P(("ctx", "fsdp")),
            P(("ctx", "fsdp"), None),
            P(("ctx", "fsdp"), None),
            P(("ctx", "fsdp"), None),
        ),
        check_vma=False,
    )
```

profile of v0, /device:TPU:6, one launch (start us, length us, event | category | flops | bytes accessed | tf_op | source)
XLA Modules:
  0.0 2393.2 jit_solution(3717252393112912097)
XLA Ops:
  11.3 40.7 %all-reduce.3 = (bf16[1536]{0:T(1024)(128)(2,1)S(1)}, bf16[128]{0:T(256)(128)(2,1)S(1)}, bf16[1536]{0:T(1024)(128)(2,1)S(1)}) all-reduce(bf16[1536]{0:T(1024)(128)(2,1)S(1)} %dynamic-update-slice, bf16[128]{0:T(256)(128)(2,1)S(1)} %dynamic-update-slice.1, ...), channel_id=1, replica_groups=mesh['ctx'=8,'fsdp'=4] {'ctx','fsdp'}, use_global_device_ids=true, to_apply=%add | all-reduce | flops 3200 | bytes 12800
  54.6 11.8 all-gather.10.cloned.1.call-done
  71.4 51.8 %all-gather.16.cloned.1.call-done = bf16[1536,512]{1,0:T(8,128)(2,1)} async-done(((bf16[48,512]{1,0:T(8,128)(2,1)}), bf16[1536,512]{1,0:T(8,128)(2,1)}) %all-gather.16.cloned.1.call-update) | async-done | bytes 1572880 | tf_op jit(solution)/shard_map/all_gather | solution.py:123
  131.1 33.9 %all-gather.12.cloned.1.call-done = bf16[1024,512]{1,0:T(8,128)(2,1)} async-done(((bf16[128,512]{1,0:T(8,128)(2,1)}), bf16[1024,512]{1,0:T(8,128)(2,1)}) %all-gather.12.cloned.1.call-update) | async-done | bytes 1048592 | tf_op jit(solution)/shard_map/all_gather | solution.py:216
  166.5 40.0 %all-gather.18.cloned.1.call-done = bf16[1024,512]{1,0:T(8,128)(2,1)} async-done(((bf16[128,512]{1,0:T(8,128)(2,1)}), bf16[1024,512]{1,0:T(8,128)(2,1)}) %all-gather.18.cloned.1.call-update) | async-done | bytes 1048592 | tf_op jit(solution)/shard_map/all_gather | solution.py:217
  208.0 63.6 %all-gather.14.cloned.1.call-done = bf16[1536,1536]{1,0:T(8,128)(2,1)} async-done(((bf16[48,1536]{1,0:T(8,128)(2,1)}), bf16[1536,1536]{1,0:T(8,128)(2,1)}) %all-gather.14.cloned.1.call-update) | async-done | bytes 4718608 | tf_op jit(solution)/shard_map/all_gather | solution.py:121
  283.4 15.8 while.45
  300.2 21.1 while.46
  322.9 14.0 all-gather.20.cloned.1.call-done
  341.2 100.8 %all-gather.22.cloned.1.call-done = bf16[1536,4608]{1,0:T(8,128)(2,1)} async-done(((bf16[48,4608]{1,0:T(8,128)(2,1)}), bf16[1536,4608]{1,0:T(8,128)(2,1)}) %all-gather.22.cloned.1.call-update) | async-done | bytes 14155792 | tf_op jit(solution)/shard_map/all_gather | solution.py:126
  441.9 8.5 fusion.96
  450.4 95.8 %all-gather.24.cloned.1.call-done = bf16[1536,4608]{1,0:T(8,128)(2,1)} async-done(((bf16[48,4608]{1,0:T(8,128)(2,1)}), bf16[1536,4608]{1,0:T(8,128)(2,1)}) %all-gather.24.cloned.1.call-update) | async-done | bytes 14155792 | tf_op jit(solution)/shard_map/all_gather | solution.py:127
  546.2 8.5 fusion.97
  554.7 95.8 %all-gather.26.cloned.1.call-done = bf16[4608,1536]{1,0:T(8,128)(2,1)} async-done(((bf16[144,1536]{1,0:T(8,128)(2,1)}), bf16[4608,1536]{1,0:T(8,128)(2,1)}) %all-gather.26.cloned.1.call-update) | async-done | bytes 14155792 | tf_op jit(solution)/shard_map/all_gather | solution.py:128
  650.5 13.1 multiply_convert_fusion
  663.6 11.0 fusion.98
  674.6 11.7 multiply_reduce_fusion
  695.3 57.1 %while.47 = (s32[]{:T(128)}, f32[128,8,3,64]{0,3,2,1:T(8,128)S(1)}, bf16[1024,512]{0,1:T(8,128)(2,1)}, bf16[1024,512]{0,1:T(8,128)(2,1)}, s32[2]{0:T(128)}, /*in...) while((s32[]{:T(128)}, f32[128,8,3,64]{0,3,2,1:T(8,128)S(1)}, ...), condition=%wide.region_27.28_spmd, body=%wide.region_22.27_spmd.sunk | while | flops 1023187968 | bytes 65619024 | solution.py:96
  700.5 24.0 %conditional.8 = ((f32[128,8,3,64]{0,3,2,1:T(8,128)S(1)}, bf16[1024,512]{0,1:T(8,128)(2,1)}, bf16[1024,512]{0,1:T(8,128)(2,1)})) conditional(s32[]{:T(128)} %convert_element_type.520, (f32[128,8,3,64]{0,3,2,1:T(8,128)S(1)}, bf16[1024,512]{0,1:T(8,128)(2,1)}, bf16[1024,512]{0,1:T(8,128)(2,1)}) %tuple.165, (s32[512]{0:T(512)S(1)}, ...), branch_computations={%region_25.25_spmd, %region_26.26_spmd} | conditional | flops 1023148032 | bytes 65608408 | solution.py:88
  729.7 22.7 conditional.8
  771.2 46.1 %reduce-scatter.7.cloned.1.call-done = bf16[128,512]{1,0:T(8,128)(2,1)} async-done(((bf16[1024,512]{1,0:T(8,128)(2,1)}), bf16[128,512]{1,0:T(8,128)(2,1)}) %reduce-scatter.7.cloned.1.call-update) | async-done | bytes 131088
  828.4 55.4 %reduce-scatter.9.cloned.1.call-done = bf16[128,512]{1,0:T(8,128)(2,1)} async-done(((bf16[1024,512]{1,0:T(8,128)(2,1)}), bf16[128,512]{1,0:T(8,128)(2,1)}) %reduce-scatter.9.cloned.1.call-update) | async-done | bytes 131088
  892.8 14.1 copy.156
  907.4 11.0 reduce.4
  927.1 14.1 copy.155
  941.2 11.0 reduce.5
  954.3 9.4 all-to-all-done.3
  969.5 52.2 %copy.154 = bf16[1,1536,1536]{2,0,1:T(2,128)(2,1)} copy(bf16[1,1536,1536]{2,1,0:T(8,128)(2,1)S(1)} %fusion.44) | data formatting | bytes 9437184 | tf_op jit(solution)/shard_map/convert_element_type | solution.py:410
  1021.7 31.9 %reduce.3 = bf16[1536,1536]{1,0:T(8,128)(2,1)} reduce(bf16[1536,1,1536]{2,1,0:T(2,128)(2,1)} %bitcast.297, bf16[]{:T(256)} %broadcast.628), dimensions={1}, to_apply=%bitcast.267.reduce_sub_computation | reduce | bytes 9437186
  1053.6 8.2 reshape.617
  1070.7 52.2 %copy.153 = bf16[1,1536,1536]{2,0,1:T(2,128)(2,1)} copy(bf16[1,1536,1536]{2,1,0:T(8,128)(2,1)S(1)} %fusion.45) | data formatting | bytes 9437184 | tf_op jit(solution)/shard_map/convert_element_type | solution.py:431
  1122.9 31.9 %reduce.6 = bf16[1536,1536]{1,0:T(8,128)(2,1)} reduce(bf16[1536,1,1536]{2,1,0:T(2,128)(2,1)} %bitcast.298, bf16[]{:T(256)} %broadcast.628), dimensions={1}, to_apply=%bitcast.266.reduce_sub_computation | reduce | bytes 9437186
  1154.7 8.2 reshape.623
  1162.9 11.4 all-to-all-done.2
  1180.7 7.1 fusion.41
  1187.8 25.2 %copy.152 = bf16[1,1536,4608]{2,0,1:T(2,128)(2,1)} copy(bf16[1,1536,4608]{2,1,0:T(8,128)(2,1)} %fusion.41) | data formatting | bytes 28311552 | tf_op jit(solution)/shard_map/convert_element_type | solution.py:445
  1213.0 90.9 %reduce.7 = bf16[1536,4608]{1,0:T(8,128)(2,1)} reduce(bf16[1536,1,4608]{2,1,0:T(2,128)(2,1)} %bitcast.291, bf16[]{:T(256)} %broadcast.628), dimensions={1}, to_apply=%bitcast.265.reduce_sub_computation | reduce | bytes 28311554
  1303.9 25.9 %reshape.625 = bf16[32,2,110592]{2,1,0:T(2,128)(2,1)} reshape(bf16[1536,4608]{1,0:T(8,128)(2,1)} %reduce.7) | data formatting | bytes 28311552
  1343.2 25.2 %copy.151 = bf16[1,1536,4608]{2,0,1:T(2,128)(2,1)} copy(bf16[1,1536,4608]{2,1,0:T(8,128)(2,1)} %fusion.42) | data formatting | bytes 28311552 | tf_op jit(solution)/shard_map/convert_element_type | solution.py:452
  1368.4 90.9 %reduce.8 = bf16[1536,4608]{1,0:T(8,128)(2,1)} reduce(bf16[1536,1,4608]{2,1,0:T(2,128)(2,1)} %bitcast.292, bf16[]{:T(256)} %broadcast.628), dimensions={1}, to_apply=%bitcast.264.reduce_sub_computation | reduce | bytes 28311554
  1459.3 25.9 %reshape.627 = bf16[32,2,110592]{2,1,0:T(2,128)(2,1)} reshape(bf16[1536,4608]{1,0:T(8,128)(2,1)} %reduce.8) | data formatting | bytes 28311552
  1485.1 170.5 %all-to-all-done.7 = bf16[32,2,110592]{2,1,0:T(2,128)(2,1)} async-done(((bf16[32,2,110592]{2,1,0:T(2,128)(2,1)}), bf16[32,2,110592]{2,1,0:T(2,128)(2,1)}, u32[]{:S(2)}, u32[]{:S(2)}) %all-to-all-start.7) | async-done | bytes 14155808 | tf_op jit(solution)/shard_map/all_to_all | solution.py:444
  1659.4 7.1 fusion.43
  1666.5 25.2 %copy.150 = bf16[1,4608,1536]{2,0,1:T(2,128)(2,1)} copy(bf16[1,4608,1536]{2,1,0:T(8,128)(2,1)} %fusion.43) | data formatting | bytes 28311552 | tf_op jit(solution)/shard_map/convert_element_type | solution.py:459
  1691.7 90.8 %reduce.9 = bf16[4608,1536]{1,0:T(8,128)(2,1)} reduce(bf16[4608,1,1536]{2,1,0:T(2,128)(2,1)} %bitcast.290, bf16[]{:T(256)} %broadcast.628), dimensions={1}, to_apply=%bitcast.263.reduce_sub_computation | reduce | bytes 28311554
  1782.5 26.0 %reshape.629 = bf16[32,2,110592]{2,1,0:T(2,128)(2,1)} reshape(bf16[4608,1536]{1,0:T(8,128)(2,1)} %reduce.9) | data formatting | bytes 28311552
  1808.4 170.1 %all-to-all-done.8 = bf16[32,2,110592]{2,1,0:T(2,128)(2,1)} async-done(((bf16[32,2,110592]{2,1,0:T(2,128)(2,1)}), bf16[32,2,110592]{2,1,0:T(2,128)(2,1)}, u32[]{:S(2)}, u32[]{:S(2)}) %all-to-all-start.8) | async-done | bytes 14155808 | tf_op jit(solution)/shard_map/all_to_all | solution.py:451
  1982.5 7.9 fusion.50
  1993.9 9.5 reshape.620
  2005.7 9.5 reshape.622
  2022.7 20.2 reshape.618
  2042.9 8.4 copy.136
  2051.3 20.2 reshape.624
  2071.4 8.4 copy.139
  2089.8 29.0 %reshape.626 = bf16[1536,1,4608]{2,1,0:T(2,128)(2,1)} reshape(bf16[32,2,110592]{2,1,0:T(2,128)(2,1)} %all-to-all-done.7) | data formatting | bytes 28311552
  2118.8 23.1 copy.140
  2141.9 29.0 %reshape.628 = bf16[1536,1,4608]{2,1,0:T(2,128)(2,1)} reshape(bf16[32,2,110592]{2,1,0:T(2,128)(2,1)} %all-to-all-done.8) | data formatting | bytes 28311552
  2170.9 23.1 copy.141
  2194.0 107.5 %all-to-all-done.9 = bf16[32,2,110592]{2,1,0:T(2,128)(2,1)} async-done(((bf16[32,2,110592]{2,1,0:T(2,128)(2,1)}), bf16[32,2,110592]{2,1,0:T(2,128)(2,1)}, u32[]{:S(2)}, u32[]{:S(2)}) %all-to-all-start.9) | async-done | bytes 14155808 | tf_op jit(solution)/shard_map/all_to_all | solution.py:458
  2301.5 29.3 %reshape.630 = bf16[4608,1,1536]{2,1,0:T(2,128)(2,1)} reshape(bf16[32,2,110592]{2,1,0:T(2,128)(2,1)} %all-to-all-done.9) | data formatting | bytes 28311552
  2330.8 23.3 copy.142
  2354.1 10.7 reduce_sum.283
  2364.8 10.7 reduce_sum.284
  2375.5 10.7 reduce_sum.285
  (331 shorter events, 262.2 us)
Async XLA Ops:
  7.2 116.0 %copy-start.1 = (bf16[1,128,1536]{2,1,0:T(8,128)(2,1)S(1)}, bf16[1,128,1536]{2,1,0:T(8,128)(2,1)}, u32[]{:S(2)}) copy-start(bf16[1,128,1536]{2,1,0:T(8,128)(2,1)} %param.26) | copy-start | bytes 1179652
  7.2 59.2 %all-gather.10.cloned.1.call-start = ((), (), s32[]{:S(2)}) async-start(), calls=%async_computation.12 | async-start | bytes 1622016 | tf_op jit(solution)/shard_map/all_gather | solution.py:122
  7.9 115.3 %all-gather.16.cloned.1.call-start = ((), (), s32[]{:S(2)}) async-start(), calls=%async_computation.15 | async-start | bytes 1622016 | tf_op jit(solution)/shard_map/all_gather | solution.py:123
  8.7 156.4 %all-gather.12.cloned.1.call-start = ((), (), s32[]{:S(2)}) async-start(), calls=%async_computation.13 | async-start | bytes 1179648 | tf_op jit(solution)/shard_map/all_gather | solution.py:216
  52.0 916.0 %copy-start.32 = (f32[1536]{0:T(1024)}, f32[1536]{0:T(1024)S(1)}, u32[]{:S(2)}) copy-start(f32[1536]{0:T(1024)S(1)} %convert_element_type.307) | copy-start | bytes 18436
  54.3 224.0 %copy-start.47 = (f32[128]{0:T(128)}, f32[128]{0:T(128)S(1)}, u32[]{:S(2)}) copy-start(f32[128]{0:T(128)S(1)} %get-tuple-element.945) | copy-start | bytes 1540
  54.4 71.9 %copy-start.57 = (f32[64]{0:T(128)}, f32[64]{0:T(128)S(1)}, u32[]{:S(2)}) copy-start(f32[64]{0:T(128)S(1)} %get-tuple-element.949) | copy-start | bytes 772
  54.4 228.4 %copy-start.55 = (f32[64]{0:T(128)}, f32[64]{0:T(128)S(1)}, u32[]{:S(2)}) copy-start(f32[64]{0:T(128)S(1)} %get-tuple-element.948) | copy-start | bytes 772
  54.6 228.4 %copy-start.35 = (f32[128,32]{0,1:T(8,128)}, f32[128,32]{0,1:T(8,128)S(1)}, u32[]{:S(2)}) copy-start(f32[128,32]{0,1:T(8,128)S(1)} %get-tuple-element.942) | copy-start | bytes 49156
  54.6 228.4 %copy-start.37 = (f32[128,32]{0,1:T(8,128)}, f32[128,32]{0,1:T(8,128)S(1)}, u32[]{:S(2)}) copy-start(f32[128,32]{0,1:T(8,128)S(1)} %get-tuple-element.943) | copy-start | bytes 49156
  69.7 136.8 %copy-start.21 = (f32[128,8,64]{0,2,1:T(8,128)}, f32[128,8,64]{0,2,1:T(8,128)S(1)}, u32[]{:S(2)}) copy-start(f32[128,8,64]{0,2,1:T(8,128)S(1)} %get-tuple-element.951) | copy-start | bytes 786436
  70.4 137.7 %copy-start.41 = (f32[128,8]{0,1:T(8,128)}, f32[128,8]{0,1:T(8,128)S(1)}, u32[]{:S(2)}) copy-start(f32[128,8]{0,1:T(8,128)S(1)} %get-tuple-element.941) | copy-start | bytes 12292
  71.3 135.2 %all-gather.18.cloned.1.call-start = ((), (), s32[]{:S(2)}) async-start(), calls=%async_computation.16 | async-start | bytes 1179648 | tf_op jit(solution)/shard_map/all_gather | solution.py:217
  125.7 145.9 %all-gather.14.cloned.1.call-start = ((), (), s32[]{:S(2)}) async-start(), calls=%async_computation.14 | async-start | bytes 4866048 | tf_op jit(solution)/shard_map/all_gather | solution.py:121
  126.3 210.6 %all-gather.20.cloned.1.call-start = ((), (), s32[]{:S(2)}) async-start(), calls=%async_computation.17 | async-start | bytes 4866048 | tf_op jit(solution)/shard_map/all_gather | solution.py:124
  126.9 315.0 %all-gather.22.cloned.1.call-start = ((), (), s32[]{:S(2)}) async-start(), calls=%async_computation.18 | async-start | bytes 14598144 | tf_op jit(solution)/shard_map/all_gather | solution.py:126
  127.6 418.6 %all-gather.24.cloned.1.call-start = ((), (), s32[]{:S(2)}) async-start(), calls=%async_computation.19 | async-start | bytes 14598144 | tf_op jit(solution)/shard_map/all_gather | solution.py:127
  128.4 522.2 %all-gather.26.cloned.1.call-start = ((), (), s32[]{:S(2)}) async-start(), calls=%async_computation.20 | async-start | bytes 14598144 | tf_op jit(solution)/shard_map/all_gather | solution.py:128
  129.1 688.1 %reduce-scatter.7.cloned.1.call-start = ((), (), s32[]{:S(2)}) async-start(), calls=%async_computation.21 | async-start | bytes 1179648
  321.3 129.1 %copy-start.3 = (bf16[2,512,512]{1,2,0:T(8,128)(2,1)}, bf16[2,512,512]{1,2,0:T(8,128)(2,1)S(1)}, u32[]{:S(2)}) copy-start(bf16[2,512,512]{1,2,0:T(8,128)(2,1)S(1)} %get-tuple-element.1326) | copy-start | bytes 3145732
  321.3 129.1 %copy-start.53 = (f32[8,3,128]{2,1,0:T(4,128)}, f32[8,3,128]{2,1,0:T(4,128)S(1)}, u32[]{:S(2)}) copy-start(f32[8,3,128]{2,1,0:T(4,128)S(1)} %get-tuple-element.1371) | copy-start | bytes 36868
  322.9 17.2 copy-start.16
  546.2 104.3 %copy-start.30 = (bf16[1,128,1536]{2,1,0:T(8,128)(2,1)S(1)}, bf16[1,128,1536]{2,1,0:T(8,128)(2,1)}, u32[]{:S(2)}) copy-start(bf16[1,128,1536]{2,1,0:T(8,128)(2,1)} %param.27) | copy-start | bytes 1179652
  663.6 11.0 copy-start.5
  663.6 11.0 copy-start.18
  663.6 25.0 %slice-start = ((s8[4718592]{0:T(1024)(128)(4,1)}), s8[4194304]{0:T(1024)(128)(4,1)S(1)}, s32[]{:S(2)}) async-start(s8[4718592]{0:T(1024)(128)(4,1)} %bitcast.303), calls=%async_computation.23 | async-start | bytes 8388608
  674.6 14.0 slice-start.1
  757.3 6.7 copy-start.25
  759.0 64.9 %all-to-all-start.6 = ((bf16[1,32,48]{2,0,1:T(2,128)(2,1)}), bf16[1,32,48]{2,0,1:T(2,128)(2,1)}, u32[]{:S(2)}, u32[]{:S(2)}) async-start(bf16[1,32,48]{2,0,1:T(2,128)(2,1)} %convert_element_type.380), calls=%async_computation.6 | async-start | bytes 32768 | tf_op jit(solution)/shard_map/all_to_all | solution.py:437
  763.2 120.6 %reduce-scatter.9.cloned.1.call-start = ((), (), s32[]{:S(2)}) async-start(), calls=%async_computation.22 | async-start | bytes 1179648
  763.9 55.1 %copy-start.22 = (f32[128,8,64]{0,2,1:T(8,128)S(1)}, f32[128,8,64]{0,2,1:T(8,128)}, u32[]{:S(2)}) copy-start(f32[128,8,64]{0,2,1:T(8,128)} %copy-done.21) | copy-start | bytes 786436
  764.0 55.1 %copy-start.42 = (f32[128,8]{0,1:T(8,128)S(1)}, f32[128,8]{0,1:T(8,128)}, u32[]{:S(2)}) copy-start(f32[128,8]{0,1:T(8,128)} %copy-done.41) | copy-start | bytes 12292
  764.0 56.8 %copy-start.14 = (bf16[1536,512]{1,0:T(8,128)(2,1)S(1)}, bf16[1536,512]{1,0:T(8,128)(2,1)}, u32[]{:S(2)}) copy-start(bf16[1536,512]{1,0:T(8,128)(2,1)} %all-gather.10.cloned.1.call-done) | copy-start | bytes 4718596
  765.5 55.2 %copy-start.51 = (f32[128,8]{0,1:T(8,128)S(1)}, f32[128,8]{0,1:T(8,128)}, u32[]{:S(2)}) copy-start(f32[128,8]{0,1:T(8,128)} %get-tuple-element.940) | copy-start | bytes 12292
  765.5 55.2 %copy-start.58 = (f32[64]{0:T(128)S(1)}, f32[64]{0:T(128)}, u32[]{:S(2)}) copy-start(f32[64]{0:T(128)} %copy-done.57) | copy-start | bytes 772
  766.2 117.6 %copy-start.48 = (f32[128]{0:T(128)S(1)}, f32[128]{0:T(128)}, u32[]{:S(2)}) copy-start(f32[128]{0:T(128)} %copy-done.47) | copy-start | bytes 1540
  823.9 64.1 %all-to-all-start.1 = ((bf16[1,32,4]{2,0,1:T(2,128)(2,1)}), bf16[1,32,4]{2,0,1:T(2,128)(2,1)S(1)}, u32[]{:S(2)}, u32[]{:S(2)}) async-start(bf16[1,32,4]{2,0,1:T(2,128)(2,1)} %copy.112), calls=%async_computation.1 | async-start | bytes 32768 | tf_op jit(solution)/shard_map/all_to_all | solution.py:402
  888.1 18.8 copy-start.43
  888.1 32.5 %all-to-all-start = ((bf16[1,32,48]{2,0,1:T(2,128)(2,1)}), bf16[1,32,48]{2,0,1:T(2,128)(2,1)S(1)}, u32[]{:S(2)}, u32[]{:S(2)}) async-start(bf16[1,32,48]{2,0,1:T(2,128)(2,1)} %convert_element_type.379), calls=%async_computation | async-start | bytes 32768 | tf_op jit(solution)/shard_map/all_to_all | solution.py:395
  907.4 19.0 copy-start.34
  920.5 20.7 copy-start.45
  920.5 43.2 %all-to-all-start.3 = ((bf16[32,2,12288]{2,1,0:T(2,128)(2,1)}), bf16[32,2,12288]{2,1,0:T(2,128)(2,1)}, u32[]{:S(2)}, u32[]{:S(2)}) async-start(bf16[32,2,12288]{2,1,0:T(2,128)(2,1)} %reshape.619), calls=%async_computation.3 | async-start | bytes 3145728 | tf_op jit(solution)/shard_map/all_to_all | solution.py:416
  941.2 26.8 %copy-start.24 = (bf16[128,24,64]{0,2,1:T(8,128)(2,1)S(1)}, bf16[128,24,64]{0,2,1:T(8,128)(2,1)}, u32[]{:S(2)}) copy-start(bf16[128,24,64]{0,2,1:T(8,128)(2,1)} %copy-done.23) | copy-start | bytes 1179652
  963.7 98.1 %all-to-all-start.4 = ((bf16[32,2,12288]{2,1,0:T(2,128)(2,1)}), bf16[32,2,12288]{2,1,0:T(2,128)(2,1)S(1)}, u32[]{:S(2)}, u32[]{:S(2)}) async-start(bf16[32,2,12288]{2,1,0:T(2,128)(2,1)} %reshape.621), calls=%async_computation.4 | async-start | bytes 3145728 | tf_op jit(solution)/shard_map/all_to_all | solution.py:423
  1061.8 7.5 copy-start.10
  1061.8 7.5 copy-start.17
  1063.0 111.4 %all-to-all-start.2 = ((bf16[32,2,36864]{2,1,0:T(2,128)(2,1)}), bf16[32,2,36864]{2,1,0:T(2,128)(2,1)}, u32[]{:S(2)}, u32[]{:S(2)}) async-start(bf16[32,2,36864]{2,1,0:T(2,128)(2,1)} %reshape.617), calls=%async_computation.2 | async-start | bytes 9437184 | tf_op jit(solution)/shard_map/all_to_all | solution.py:409
  1162.9 17.8 copy-start.20
  1174.3 155.5 %all-to-all-start.5 = ((bf16[32,2,36864]{2,1,0:T(2,128)(2,1)}), bf16[32,2,36864]{2,1,0:T(2,128)(2,1)}, u32[]{:S(2)}, u32[]{:S(2)}) async-start(bf16[32,2,36864]{2,1,0:T(2,128)(2,1)} %reshape.623), calls=%async_computation.5 | async-start | bytes 9437184 | tf_op jit(solution)/shard_map/all_to_all | solution.py:430
  1329.8 325.8 %all-to-all-start.7 = ((bf16[32,2,110592]{2,1,0:T(2,128)(2,1)}), bf16[32,2,110592]{2,1,0:T(2,128)(2,1)}, u32[]{:S(2)}, u32[]{:S(2)}) async-start(bf16[32,2,110592]{2,1,0:T(2,128)(2,1)} %reshape.625), calls=%async_computation.7 | async-start | bytes 28311552 | tf_op jit(solution)/shard_map/all_to_all | solution.py:444
  1485.1 174.3 %copy-start.12 = (bf16[128,4608]{1,0:T(8,128)(2,1)S(1)}, bf16[128,4608]{1,0:T(8,128)(2,1)}, u32[]{:S(2)}) copy-start(bf16[128,4608]{1,0:T(8,128)(2,1)} %get-tuple-element.929) | copy-start | bytes 3538948
  1485.1 174.3 %copy-start.31 = (bf16[1,128,1536]{2,1,0:T(8,128)(2,1)S(1)}, bf16[1,128,1536]{2,1,0:T(8,128)(2,1)}, u32[]{:S(2)}) copy-start(bf16[1,128,1536]{2,1,0:T(8,128)(2,1)} %param.27) | copy-start | bytes 1179652
  1655.6 323.0 %all-to-all-start.8 = ((bf16[32,2,110592]{2,1,0:T(2,128)(2,1)}), bf16[32,2,110592]{2,1,0:T(2,128)(2,1)}, u32[]{:S(2)}, u32[]{:S(2)}) async-start(bf16[32,2,110592]{2,1,0:T(2,128)(2,1)} %reshape.627), calls=%async_computation.8 | async-start | bytes 28311552 | tf_op jit(solution)/shard_map/all_to_all | solution.py:451
  1808.4 173.9 %copy-start.6 = (f32[128,1536]{1,0:T(8,128)S(1)}, f32[128,1536]{1,0:T(8,128)}, u32[]{:S(2)}) copy-start(f32[128,1536]{1,0:T(8,128)} %copy-done.4) | copy-start | bytes 2359300
  1978.6 323.0 %all-to-all-start.9 = ((bf16[32,2,110592]{2,1,0:T(2,128)(2,1)}), bf16[32,2,110592]{2,1,0:T(2,128)(2,1)}, u32[]{:S(2)}, u32[]{:S(2)}) async-start(bf16[32,2,110592]{2,1,0:T(2,128)(2,1)} %reshape.629), calls=%async_computation.9 | async-start | bytes 28311552 | tf_op jit(solution)/shard_map/all_to_all | solution.py:458
  1982.4 9.3 copy-start.60
  1982.4 9.3 copy-start.2
  1982.4 9.3 copy-start.11
  1982.4 9.3 copy-start.27
  1982.4 9.3 copy-start.33
  1982.4 9.3 copy-start.49
  1982.5 9.3 copy-start.59
  1982.5 10.4 copy-start.44
  1982.5 10.9 copy-start.46
  (25 other events, 75.5 us)
Sparse Core Ops, SparseCore 0:
  10.9 55.4 all-gather.9
  69.2 53.9 all-gather.15
  125.9 39.0 all-gather.11
  167.6 38.8 all-gather.17
  209.3 62.3 all-gather.13
  274.4 62.4 all-gather.19
  339.8 102.0 all-gather.21
  444.8 101.3 all-gather.23
  549.2 101.3 all-gather.25
  754.9 62.2 reduce-scatter.6
  821.0 62.6 reduce-scatter.8
where the time goes:
time: 2410 us; the launch traced here: 2390 us
  waiting for transfers between devices  1080 us (45%)
  local copies, waits for them, and re-layouts  612 us (25%)
  other arithmetic  443 us (18%)
  matrix products  137 us (6%)
  starting transfers between devices  49.7 us (2%)
  blocking collectives  40.7 us (2%)
    unnamed x8, other arithmetic  358 us
    unnamed x147, local copies, waits for them, and re-layouts  350 us
    all_to_all x1, waiting for transfers between devices, on_device(): lax.all_to_all(grad_w_gate[None].astype(jnp.bfloat16), ('ctx', 'fsdp'), s...  170 us
    all_to_all x1, waiting for transfers between devices, on_device(): lax.all_to_all(grad_w_up[None].astype(jnp.bfloat16), ('ctx', 'fsdp'), spl...  170 us
    all_to_all x1, waiting for transfers between devices, on_device(): lax.all_to_all(grad_w_down[None].astype(jnp.bfloat16), ('ctx', 'fsdp'), s...  108 us
    unnamed x13, waiting for transfers between devices  107 us
    all_gather x1, waiting for transfers between devices, on_device(): lax.all_gather(w_gate, ('ctx', 'fsdp'), axis=0, tiled=True)  101 us
    all_gather x1, waiting for transfers between devices, on_device(): lax.all_gather(w_down, ('ctx', 'fsdp'), axis=0, tiled=True)  95.8 us
  transfers between devices with their start and end apart: 21, of which 16 were waited for; matrix products, arithmetic and copies ran while one was open for 42% of the time, Pallas kernels for 0%

commit v1 on v0

--- a/solution.py
+++ b/solution.py
@@ -3,6 +3,8 @@
 import jax
 import jax.numpy as jnp
 from jax import lax
+from jax.experimental import pallas as pl
+from jax.experimental.pallas import tpu as pltpu
 from jax.sharding import PartitionSpec as P
 
 QUERY_HEADS = 24
@@ -97,7 +99,7 @@
     return state
 
 
-def on_device(
+def general_plan(
     hidden_in,
     cotangent,
     block_order,
@@ -480,9 +482,1365 @@
     )
 
 
+MESH = pl.DeviceIdType.MESH
+RANKS = 8
+GROUP = QUERY_HEADS // KEY_VALUE_HEADS
+COLS = 384
+NOTES = 320
+PIECES = 4
+FIRST_UNITS = 256
+VMEM_BYTES = 60 * 1024 * 1024
+
+
+class Place:
+    def __init__(self):
+        self.ctx, self.fsdp = lax.axis_index("ctx"), lax.axis_index("fsdp")
+        self.half, self.chip = self.ctx // 4, self.ctx % 4
+        self.y, self.core = self.fsdp // 2, self.fsdp % 2
+        self.rank = self.core * 4 + self.chip
+        self.mate = (self.ctx, self.y * 2 + 1 - self.core)
+        self.y_peer = (self.ctx, (1 - self.y) * 2 + self.core)
+        self.z_peer = ((1 - self.half) * 4 + self.chip, self.fsdp)
+        self.swap_peer = ((1 - self.half) * 4 + self.chip, self.y * 2 + 1 - self.core)
+        self.stays = self.core == self.half
+        self.moves = self.core != self.half
+
+    def chip_at(self, turn):
+        low, high = self.chip % 2, self.chip // 2
+        low = 1 - low if turn % 2 else low
+        high = 1 - high if turn // 2 else high
+        return high * 2 + low
+
+    def beside(self, turn):
+        low, high = self.chip % 2, self.chip // 2
+        low = low + turn % 2 * (1 - 2 * low)
+        high = high + turn // 2 * (1 - 2 * high)
+        chip = high * 2 + low
+        return [self.core * 4 + chip, (1 - self.core) * 4 + chip]
+
+    def member(self, turn, other):
+        chip = self.chip_at(turn)
+        core = 1 - self.core if other else self.core
+        return (self.half * 4 + chip, self.y * 2 + core), chip, core
+
+    def members(self):
+        return [self.member(turn, other) for turn in range(4) for other in range(2) if turn or other]
+
+    def ranks(self, turn):
+        chip = self.chip_at(turn)
+        return self.core * 4 + chip, (1 - self.core) * 4 + chip
+
+
+class Links:
+    def __init__(self, send, receive):
+        self.send, self.receive, self.used = send, receive, 0
+
+    def link(self, source, target, device):
+        at = self.used
+        self.used += 1
+        assert at < self.send.shape[0], "semaphores"
+        return pltpu.make_async_remote_copy(
+            src_ref=source,
+            dst_ref=target,
+            send_sem=self.send.at[at],
+            recv_sem=self.receive.at[at],
+            device_id=device,
+            device_id_type=MESH,
+        )
+
+
+def greet(devices):
+    barrier = pltpu.get_barrier_semaphore()
+    for device in devices:
+        pl.semaphore_signal(barrier, inc=1, device_id=device, device_id_type=MESH)
+    pl.semaphore_wait(barrier, len(devices))
+
+
+class Spread:
+    def __init__(self, place, links, rows, block, by_x=PIECES):
+        size = rows.shape[1] // PIECES
+
+        def piece(rank, at):
+            return rows.at[rank, pl.ds(at * size, size)]
+
+        own = place.rank
+        x_rank, z_rank, far_rank = (place.ranks(turn)[0] for turn in (1, 2, 3))
+        x_device, z_device = place.member(1, 0)[0], place.member(2, 0)[0]
+        self.order_z = list(range(PIECES))
+        self.order_x = self.order_z[by_x:] + self.order_z[:by_x]
+        self.by_x, self.pieces = by_x, []
+        for at in range(PIECES):
+            source = block.at[pl.ds(at * size, size)]
+            last, device = (z_rank, x_device) if at < by_x else (x_rank, z_device)
+            self.pieces.append(
+                dict(
+                    near=links.link(source, piece(own, at), place.mate),
+                    x=links.link(source, piece(own, at), x_device),
+                    z=links.link(source, piece(own, at), z_device),
+                    on=links.link(piece(last, at), piece(last, at), device),
+                    x_mate=links.link(piece(x_rank, at), piece(x_rank, at), place.mate),
+                    z_mate=links.link(piece(z_rank, at), piece(z_rank, at), place.mate),
+                    far_mate=links.link(piece(far_rank, at), piece(far_rank, at), place.mate),
+                )
+            )
+
+    def start(self):
+        for at_z, at_x in zip(self.order_z, self.order_x):
+            self.pieces[at_z]["z"].start()
+            self.pieces[at_x]["x"].start()
+        for piece in self.pieces:
+            piece["near"].start()
+
+    def start_piece(self, at):
+        for name in ("z", "x", "near"):
+            self.pieces[at][name].start()
+
+    def relay(self, steps=range(PIECES)):
+        for step in steps:
+            at_z, at_x = self.order_z[step], self.order_x[step]
+            self.pieces[at_z]["z"].wait_recv()
+            if at_z < self.by_x:
+                self.pieces[at_z]["on"].start()
+            self.pieces[at_z]["z_mate"].start()
+            self.pieces[at_x]["x"].wait_recv()
+            if at_x >= self.by_x:
+                self.pieces[at_x]["on"].start()
+            self.pieces[at_x]["x_mate"].start()
+
+    def relay_far(self):
+        for piece in self.pieces:
+            piece["on"].wait_recv()
+            piece["far_mate"].start()
+
+    def arrive(self, names=("near", "x_mate", "z_mate", "far_mate")):
+        for piece in self.pieces:
+            for name in names:
+                piece[name].wait_recv()
+
+    def finish(self):
+        for piece in self.pieces:
+            for copy in piece.values():
+                copy.wait_send()
+
+
+class Collect:
+    def __init__(self, place, links, part, near, out, into, out_last, into_last):
+        self.place, self.part, self.near = place, part, near
+        self.out, self.into, self.out_last, self.into_last = out, into, out_last, into_last
+        self.size = part.shape[1] // PIECES
+        x_device, z_device = place.member(1, 0)[0], place.member(2, 0)[0]
+        self.near_links, self.first, self.last, self.near_done = {}, [], [], False
+        for turn in (3, 1, 2, 0):
+            other = place.ranks(turn)[1]
+            self.near_links[turn] = links.link(part.at[other], near.at[turn], place.mate)
+        for at in range(PIECES):
+            block, here = self.two_pieces(at)
+            self.first.append(links.link(out.at[block, here], into.at[block, here], x_device))
+            here = self.rows(at)
+            self.last.append(links.link(out_last.at[here], into_last.at[here], z_device))
+
+    def two_pieces(self, at, which=None):
+        start = at % 2 * 2 * self.size
+        if which is None:
+            return at // 2, pl.ds(start, 2 * self.size)
+        return at // 2, pl.ds(start + which * self.size, self.size)
+
+    def finish_near(self):
+        self.near_done = True
+        for copy in self.near_links.values():
+            copy.wait_send()
+
+    def send_near(self, turn):
+        self.near_links[turn].start()
+
+    def begin(self, turns=(3, 1, 2, 0)):
+        for turn in turns:
+            self.send_near(turn)
+
+    def rows(self, at):
+        return pl.ds(at * self.size, self.size)
+
+    def sum_of(self, turn, at):
+        mine = self.part[self.place.ranks(turn)[0], self.rows(at)].astype(jnp.float32)
+        return mine + self.near[turn, self.rows(at)].astype(jnp.float32)
+
+    def first_step(self):
+        for turn in (3, 1):
+            self.near_links[turn].wait_recv()
+        for at in range(PIECES):
+            for which, turn in enumerate((1, 3)):
+                self.out[self.two_pieces(at, which)] = self.sum_of(turn, at).astype(jnp.bfloat16)
+            self.first[at].start()
+
+    def second_step(self, sums):
+        for turn in (2, 0):
+            self.near_links[turn].wait_recv()
+        for at in range(PIECES):
+            self.first[at].wait_recv()
+            total = self.sum_of(2, at) + self.into[self.two_pieces(at, 1)].astype(jnp.float32)
+            self.out_last[self.rows(at)] = total.astype(jnp.bfloat16)
+            self.last[at].start()
+            total = self.sum_of(0, at) + self.into[self.two_pieces(at, 0)].astype(jnp.float32)
+            sums[self.rows(at)] = total
+
+    def third_step(self, sums, then=None):
+        for at in range(PIECES):
+            self.last[at].wait_recv()
+            sums[self.rows(at)] += self.into_last[self.rows(at)].astype(jnp.float32)
+            if then is not None:
+                then(at, self.rows(at))
+
+    def finish(self):
+        if not self.near_done:
+            self.finish_near()
+        for first, last in zip(self.first, self.last):
+            first.wait_send()
+            last.wait_send()
+
+
+def collect_scratch(rows, width):
+    return [pltpu.VMEM(count + (rows, width), jnp.bfloat16) for count in ((4,), (2,), (2,), (), ())]
+
+
+COLLECT_LINKS = 4 + 2 * PIECES
+SPREAD_LINKS = 7 * PIECES
+
+
+class Columns:
+    def __init__(self, place, links, pieces, whole, local, parts):
+        own = whole.at[place.half, place.chip, place.y, place.core]
+        self.own = pltpu.make_async_copy(pieces.at[place.chip, place.core], own, local)
+        self.square = [
+            links.link(pieces.at[chip, core], own, device)
+            for device, chip, core in place.members()
+        ]
+        self.z, self.y, self.y_second = [], [], []
+        for lanes in parts:
+            here = whole.at[place.half, :, place.y, :, :, lanes]
+            there = whole.at[1 - place.half, :, place.y, :, :, lanes]
+            self.z.append(links.link(here, here, place.z_peer))
+            self.y.append(links.link(here, here, place.y_peer))
+            self.y_second.append(links.link(there, there, place.y_peer))
+
+    def start(self):
+        self.own.start()
+        for copy in self.square:
+            copy.start()
+
+    def square_done(self):
+        self.own.wait()
+        for copy in self.square:
+            copy.wait_recv()
+
+    def across(self, part=0):
+        self.z[part].start()
+        self.y[part].start()
+
+    def relay(self, part=0):
+        self.z[part].wait_recv()
+        self.y_second[part].start()
+
+    def arrive(self, part=0):
+        self.y[part].wait_recv()
+        self.y_second[part].wait_recv()
+
+    def finish(self, part=0):
+        for copy in (self.z[part], self.y[part], self.y_second[part]):
+            copy.wait_send()
+        if part == 0:
+            for copy in self.square:
+                copy.wait_send()
+
+
+class Rows:
+    def __init__(self, place, links, block, whole, local):
+        own, pair = whole.at[place.y, place.core], whole.at[place.y]
+        self.place = place
+        self.own = pltpu.make_async_copy(block, own, local)
+        self.mate = links.link(block, own, place.mate)
+        self.z = links.link(pair, pair, place.z_peer)
+        self.y = links.link(pair, pair, place.y_peer)
+
+    def start(self):
+        pl.when(self.place.stays)(self.own.start)
+        pl.when(self.place.moves)(self.mate.start)
+
+    def pair_done(self):
+        @pl.when(self.place.stays)
+        def _():
+            self.own.wait()
+            self.mate.wait_recv()
+            self.z.start()
+            self.y.start()
+
+    def relay(self):
+        @pl.when(self.place.moves)
+        def _():
+            self.z.wait_recv()
+            self.y.start()
+
+    def arrive(self):
+        self.y.wait_recv()
+
+    def finish(self):
+        pl.when(self.place.stays)(self.z.wait_send)
+        pl.when(self.place.moves)(self.mate.wait_send)
+        self.y.wait_send()
+
+
+def iota(dims, axis):
+    return lax.broadcasted_iota(jnp.int32, dims, axis)
+
+
+def chosen(condition):
+    return jnp.where(condition, 1.0, 0.0).astype(jnp.bfloat16)
+
+
+def dot(a, b):
+    return jnp.dot(a, b, preferred_element_type=jnp.float32)
+
+
+def dot_turned(a, b):
+    return lax.dot_general(a, b, (((1,), (1,)), ((), ())), preferred_element_type=jnp.float32)
+
+
+def dot_fine(a, b):
+    high = a.astype(jnp.bfloat16)
+    rest = (a - high.astype(jnp.float32)).astype(jnp.bfloat16)
+    return dot(high, b) + dot(rest, b)
+
+
+def dot_fine_turned(b, a):
+    high = a.astype(jnp.bfloat16)
+    rest = (a - high.astype(jnp.float32)).astype(jnp.bfloat16)
+    return dot_turned(b, high) + dot_turned(b, rest)
+
+
+def head_ones():
+    return chosen(iota((256, 256), 0) // HEAD_SIZE == iota((256, 256), 1) // HEAD_SIZE)
+
+
+def dot_rows(a, b):
+    return lax.dot_general(a, b, (((0,), (0,)), ((), ())), preferred_element_type=jnp.float32)
+
+
+def laid_out(values, row):
+    count = values.shape[1]
+    table = chosen(iota((count, 128), 1) - (NOTES - 256) == iota((count, 128), 0))
+    spread_out = dot(jnp.broadcast_to(values, (16, count)), table)
+    return jnp.where(iota((16, 128), 0) == row, spread_out, 0.0)
+
+
+def gain_rows(notes, width, rows):
+    blocks = notes.shape[0] // 16
+
+    def spread_out(at, columns, each):
+        lane = iota((128, 1), 0) - (NOTES - 256)
+        table = dot(notes[pl.ds(at, blocks, 16)].astype(jnp.bfloat16), chosen(lane == columns % each))
+        return jnp.sum(
+            jnp.where(iota((blocks, 1), 0) == columns // each, table, 0.0), axis=0, keepdims=True
+        )
+
+    column = iota((1, width), 1)
+    heads = iota((1, COLS), 1)
+    heads = heads % HEAD_SIZE + jnp.where(heads >= GROUP * HEAD_SIZE, HEAD_SIZE, 0)
+    return spread_out(0, column, rows), spread_out(1, column, rows), spread_out(2, heads, 4)
+
+
+class ColumnSums:
+    def __init__(self, place, links, whole, final, y_part, far, z_part, local, parts):
+        total = y_part.at[0]
+        self.place, self.whole, self.y_part = place, whole, y_part
+        self.far, self.z_part, self.total = far, z_part, total
+        self.y, self.z, self.parts = [], [], parts
+        for lanes in parts:
+            source = whole.at[1 - place.half, :, 1 - place.y, :, :, lanes]
+            self.y.append(links.link(source, y_part.at[0, :, :, :, lanes], place.y_peer))
+            every = (slice(None), slice(None), slice(None), lanes)
+            self.z.append(links.link(far.at[every], z_part.at[every], place.z_peer))
+        source = whole.at[place.half, :, 1 - place.y]
+        self.y_near = links.link(source, y_part.at[1], place.y_peer)
+        self.own = pltpu.make_async_copy(
+            total.at[place.chip, place.core], final.at[place.rank], local
+        )
+        self.square = [
+            links.link(total.at[chip, core], final.at[place.rank], device)
+            for device, chip, core in place.members()
+        ]
+
+    def start(self, part=0):
+        self.y[part].start()
+
+    def start_near(self):
+        self.y_near.start()
+
+    def across(self, part=0):
+        self.y[part].wait_recv()
+        place, lanes = self.place, self.parts[part]
+
+        @pl.loop(0, 4)
+        def _(chip):
+            mine = self.whole[1 - place.half, chip, place.y, :, :, lanes].astype(jnp.float32)
+            both = mine + self.y_part[0, chip, :, :, lanes].astype(jnp.float32)
+            self.far[chip, :, :, lanes] = both.astype(jnp.bfloat16)
+
+        self.z[part].start()
+
+    def deal(self):
+        self.y_near.wait_recv()
+        for copy in self.z:
+            copy.wait_recv()
+        place = self.place
+
+        @pl.loop(0, 4)
+        def _(chip):
+            both = self.whole[place.half, chip, place.y].astype(jnp.float32) + self.y_part[
+                1, chip
+            ].astype(jnp.float32)
+            both = both + self.z_part[chip].astype(jnp.float32)
+            self.total[chip] = both.astype(jnp.bfloat16)
+
+        self.own.start()
+        for copy in self.square:
+            copy.start()
+
+    def finish(self):
+        self.own.wait()
+        for copy in self.square:
+            copy.wait()
+        for copy in self.y + self.z + [self.y_near]:
+            copy.wait_send()
+
+
+class RowSums:
+    def __init__(self, place, links, whole, final, y_part, pair, total):
+        z_part, last = pair, total
+        self.place, self.whole, self.final, self.y_part = place, whole, final, y_part
+        self.pair, self.z_part, self.total, self.last = pair, z_part, total, last
+        self.y = links.link(whole.at[1 - place.y], y_part, place.y_peer)
+        self.z = links.link(pair, z_part, place.z_peer)
+        self.mate = links.link(total, last, place.mate)
+
+    def start(self):
+        self.y.start()
+
+    def sum_of(self, core):
+        mine = self.whole[self.place.y, core].astype(jnp.float32)
+        return mine + self.y_part[core].astype(jnp.float32)
+
+    def across(self):
+        self.y.wait_recv()
+
+        @pl.when(self.place.moves)
+        def _():
+            for core in range(2):
+                self.pair[core] = self.sum_of(core).astype(jnp.bfloat16)
+            self.z.start()
+
+    def deal(self):
+        @pl.when(self.place.stays)
+        def _():
+            self.z.wait_recv()
+            own, other = self.place.core, 1 - self.place.core
+            both = self.sum_of(other) + self.z_part[other].astype(jnp.float32)
+            self.total[...] = both.astype(jnp.bfloat16)
+            self.mate.start()
+            self.final[...] = self.sum_of(own) + self.z_part[own].astype(jnp.float32)
+
+    def finish(self):
+        self.y.wait_send()
+
+        @pl.when(self.place.stays)
+        def _():
+            self.mate.wait_send()
+
+        @pl.when(self.place.moves)
+        def _():
+            self.z.wait_send()
+            self.mate.wait_recv()
+            self.final[...] = self.last[...].astype(jnp.float32)
+
+
+def column_scratch(block):
+    low = jnp.bfloat16
+    return [pltpu.VMEM((2, 4, 2) + block, low)] + [pltpu.VMEM((4, 2) + block, low)] * 2
+
+
+def row_scratch(block):
+    low = jnp.bfloat16
+    return [pltpu.VMEM((2,) + block, low)] * 2 + [pltpu.VMEM(block, low)]
+
+
+def norm_back(values, scale, weighted):
+    mean = jnp.mean(weighted * values, axis=-1, keepdims=True)
+    return scale * weighted - scale * scale * scale * values * mean
+
+
+def block_kernel(
+    query_w, key_w, value_w, gate_w, up_w, attn_gain, qk_gain, ffn_gain, order, positions,
+    out_w, down_w, hidden, cotangent,
+    block_out, grad_in, query_sum, key_sum, value_sum, gate_sum, up_sum, out_sum, down_sum, attn_gain_sum, ffn_gain_sum, qk_gain_sum,
+    rows, normed, two_all, branch_all, cotangent_all, heads_v, gate_up_v, out_v, down_v,
+    inner_t, unit_grad, projected, queries, keys, keys_t, values_t, mixed, mixed_t, totals,
+    index_row, index_column, tables, gains,
+    key_grad, value_grad, down_grad, scores, probs_grad, inner, gain_sums, gain_parts,
+    row_sum, grad_middle, middle, own_low, block_low, in_low, rows_own,
+    near_a, first_a, into_a, last_a, into_last_a,
+    gate_up_y, gate_up_far, gate_up_z, heads_y, heads_far, heads_z,
+    down_y, down_pair, down_t, out_y, out_pair, out_t,
+    send, receive, local,
+):
+    place, links = Place(), Links(send, receive)
+    single, low = jnp.float32, jnp.bfloat16
+    tokens, width = hidden.shape
+    span, head = RANKS * tokens, HEAD_SIZE
+    rows_of, units = query_w.shape[0], 4 * down_w.shape[0]
+    pair_rows = 2 * tokens
+    early = FIRST_UNITS
+    late = units // 128 * 128 - early
+    unit_parts = [pl.ds(0, 2 * early), pl.ds(2 * early, 2 * (units - early))]
+    set_a = (near_a, first_a, into_a, last_a, into_last_a)
+    heads_grad = unit_grad.at[:, 0:COLS]
+    part, query_grad = rows, mixed
+    probs, scores_grad = unit_grad.at[:, COLS : COLS + 256], unit_grad.at[:, COLS + 256 : COLS + 512]
+
+    def moved(source, target, at):
+        keep = pltpu.make_async_copy(source, target, local.at[at])
+        return keep, links.link(source, target, place.swap_peer)
+
+    def go(pair):
+        pl.when(place.stays)(pair[0].start)
+        pl.when(place.moves)(pair[1].start)
+
+    def come(pair):
+        pl.when(place.stays)(pair[0].wait)
+        pl.when(place.moves)(pair[1].wait)
+
+    heads_w, gate_up_w = heads_far, gate_up_far
+    notes = key_grad.at[0, 0 : 4 * RANKS * 16]
+    landing = cotangent_all.at[4:8].reshape(RANKS, tokens // 2, width)
+    heads_sum = landing.at[:, 0:rows_of, 2 * units :]
+    gate_up_sum = landing.at[:, 0:rows_of, 0 : 2 * units]
+    hidden_move = moved(hidden, rows.at[place.ctx], 0)
+    cotangent_move = moved(cotangent, cotangent_all.at[place.ctx], 1)
+    block_move = moved(block_low, block_out, 2)
+    in_move = moved(in_low, grad_in, 3)
+    heads = Columns(place, links, heads_w, heads_v, local.at[4], [pl.ds(0, COLS)])
+    out = Rows(place, links, out_w, out_v, local.at[5])
+    gate_up = Columns(place, links, gate_up_w, gate_up_v, local.at[6], unit_parts)
+    down = Rows(place, links, down_w, down_v, local.at[7])
+    hidden_spread = Spread(place, links, rows, rows.at[place.rank])
+    cotangent_spread = Spread(place, links, cotangent_all, cotangent_all.at[place.rank])
+    two_spread = Spread(place, links, two_all, own_low)
+    branch_spread = Spread(place, links, branch_all, own_low)
+    attention_collect = Collect(place, links, part, *set_a)
+    two_collect = Collect(place, links, part, *set_a)
+    down_collect = Collect(
+        place, links, part, two_all.at[0:4], two_all.at[4:6], two_all.at[6:8],
+        cotangent_all.at[0], cotangent_all.at[1],
+    )
+    last_collect = Collect(place, links, part, *set_a)
+    gate_up_sums = ColumnSums(
+        place, links, gate_up_v, gate_up_sum, gate_up_y, gate_up_far, gate_up_z, local.at[8],
+        unit_parts,
+    )
+    heads_sums = ColumnSums(
+        place, links, heads_v, heads_sum, heads_y, heads_far, heads_z, local.at[9],
+        [pl.ds(0, COLS)],
+    )
+    down_sums = RowSums(place, links, down_grad, down_sum, down_y, down_pair, down_t)
+    out_sums = RowSums(place, links, out_v, out_sum, out_y, out_pair, out_t)
+
+    greet(
+        [device for device, _, _ in place.members()]
+        + [place.y_peer, place.z_peer, place.swap_peer]
+    )
+    go(hidden_move)
+    out.start()
+    down.start()
+    first_slot = jnp.sum(
+        jnp.where(iota(order.shape, 1) == 2 * place.ctx, order[...].astype(single), 0.0),
+        axis=1,
+        keepdims=True,
+    )
+    start = positions[:, 0:1].astype(single) - 64.0 * first_slot
+    start_high = jnp.floor(start * (1.0 / 64.0))
+    note = laid_out(attn_gain[...], 0) + laid_out(ffn_gain[...], 1) + laid_out(qk_gain[...], 2)
+    note = note + laid_out(order[...].astype(single).astype(low), 3)
+    at_row, at_lane = iota((16, 128), 0), iota((16, 128), 1) - (NOTES - 256)
+    note = note + jnp.where((at_row == 4) & (at_lane == 0), start_high, 0.0)
+    note = note + jnp.where((at_row == 4) & (at_lane == 1), start - 64.0 * start_high, 0.0)
+    note = jnp.concatenate([note, jnp.zeros((rows_of - 16, 128), single)], axis=0)
+    low_part = iota((rows_of, 128), 1) < head
+    for rank in range(RANKS):
+        odd = rank % 2
+        base = rank * GROUP * head - odd * head
+        values = query_w[:, base : base + 256].astype(single)
+        values = pltpu.roll(values, 256 - head, 1) if odd else values
+        base = rank // 2 * 128
+        key, value = key_w[:, base : base + 128].astype(single), value_w[:, base : base + 128].astype(single)
+        key = key if odd else pltpu.roll(key, head, 1)
+        value = pltpu.roll(value, head, 1) if odd else value
+        piece = heads_w.at[rank % 4, rank // 4]
+        piece[:, 0:128] = values[:, 0:128].astype(low)
+        piece[:, 128:256] = jnp.where(low_part, values[:, 128:256], key).astype(low)
+        piece[:, 256:COLS] = jnp.where(low_part, value, note).astype(low)
+    heads.start()
+    for rank in range(RANKS):
+        odd = rank % 2
+        base = rank * units - odd * head
+        wide = units + head
+        both_w = []
+        for source in (gate_w, up_w):
+            values = source[:, base : base + wide].astype(single)
+            both_w.append(pltpu.roll(values, wide - head, 1) if odd else values)
+        piece, end = gate_up_w.at[rank % 4, rank // 4], early + late
+        for side, values in enumerate(both_w):
+            piece[:, side * early : (side + 1) * early] = values[:, 0:early].astype(low)
+            base = 2 * early + side * (late + 128)
+            piece[:, base : base + late] = values[:, early:end].astype(low)
+        shared = jnp.where(low_part, both_w[0][:, end:], pltpu.roll(both_w[1][:, end:], head, 1))
+        piece[:, 2 * early + late : 2 * early + late + 128] = shared.astype(low)
+    gate_up.start()
+    out_v[2] = jnp.zeros(out_v.shape[1:], low)
+    totals[...] = jnp.zeros(totals.shape, single)
+    come(hidden_move)
+    hidden_spread.start()
+    rows_own[...] = rows[place.rank]
+    heads.square_done()
+    heads.across()
+    go(cotangent_move)
+
+    note = heads_v[place.half, place.chip, place.y, place.half, 0:16, 256:COLS]
+    lane = iota((128, span), 0) - (NOTES - 256)
+    spread_out = dot(note, chosen(lane == iota((128, span), 1) // 64))
+    order_row = jnp.sum(jnp.where(iota((16, span), 0) == 3, spread_out, 0.0), axis=0, keepdims=True)
+    row = order_row * 64.0 + (iota((1, span), 1) % 64).astype(single)
+    index_row[...] = jnp.broadcast_to(row, (8, span))
+    lane = iota((span, 128), 1) - (NOTES - 256)
+    spread_out = dot_turned(chosen(lane == iota((span, 128), 0) // 64), note)
+    order_column = jnp.sum(
+        jnp.where(iota((span, 16), 1) == 3, spread_out, 0.0), axis=1, keepdims=True
+    )
+    column = order_column * 64.0 + (iota((span, 1), 0) % 64).astype(single)
+    index_column[...] = jnp.broadcast_to(column, (span, 128))
+    at_row, at_lane = iota((16, 128), 0), iota((16, 128), 1) - (NOTES - 256)
+    weight = jnp.where(at_lane == 0, 64.0, 1.0)
+    picked = jnp.where((at_row == 4) & (at_lane >= 0) & (at_lane < 2), note.astype(single), 0.0)
+    start = jnp.sum(jnp.sum(picked * weight, axis=1, keepdims=True), axis=0, keepdims=True)
+    slots = dot_turned(chosen(at_lane == at_row), note)
+    first = jnp.sum(jnp.where(iota((16, 16), 1) == 3, slots, 0.0), axis=1, keepdims=True)
+    frequency = (iota((8, 128), 1) % (head // 2)).astype(single) * (-2.0 * math.log(THETA) / head)
+    frequency = jnp.exp(frequency)[0:1]
+    first = (first * 64.0 + start) * frequency
+    second = iota((64, 128), 0).astype(single) * frequency
+    tables[0:16], tables[16:32] = jnp.cos(first), jnp.sin(first)
+    tables[32:96], tables[96:160] = jnp.cos(second), jnp.sin(second)
+
+    def rotation(at):
+        cos_b, sin_b = tables[32:96], tables[96:160]
+        first_half = (iota((64, 128), 1) % head) < head // 2
+        sin_signed = jnp.where(first_half, -sin_b, sin_b)
+        cos_signed = jnp.where(first_half, -cos_b, cos_b)
+        cosines, sines = [], []
+        for slot in range(pair_rows // 64):
+            cos_a = tables[pl.ds(at * (pair_rows // 64) + slot, 1)]
+            sin_a = tables[pl.ds(16 + at * (pair_rows // 64) + slot, 1)]
+            cosines.append(cos_a * cos_b - sin_a * sin_b)
+            sines.append(sin_a * cos_signed + cos_a * sin_signed)
+        cosine, sine = jnp.concatenate(cosines, axis=0), jnp.concatenate(sines, axis=0)
+        return jnp.concatenate([cosine] * 2, axis=1), jnp.concatenate([sine] * 2, axis=1)
+
+    hidden_spread.relay()
+    heads.relay()
+    out.pair_done()
+    gate_up.square_done()
+    hidden_spread.relay_far()
+    gate_up.across(0)
+    hidden_spread.arrive()
+    heads.arrive()
+
+    notes[...] = heads_v[:, :, :, :, 0:16, 256:COLS].reshape(notes.shape).astype(single)
+    one, second, head_gain = gain_rows(notes, width, rows_of)
+    gains[0:1] = one
+    gains[1:2] = second
+    gains[2:3, 0:COLS] = head_gain
+    ones = head_ones()
+    first_half = iota((pair_rows, 256), 1) % head < head // 2
+    low_lanes = iota((pair_rows, 128), 1) < head
+
+    def pair(at):
+        return pl.ds(pl.multiple_of(at * pair_rows, pair_rows), pair_rows)
+
+    def swapped(values):
+        return jnp.where(
+            first_half, pltpu.roll(values, 256 - head // 2, 1), pltpu.roll(values, head // 2, 1)
+        )
+
+    @pl.loop(0, RANKS // 2)
+    def _(at):
+        here = pair(at)
+        for side in range(2):
+            for step in range(0, tokens, 32):
+                row = rows[at * 2 + side, step : step + 32].astype(single)
+                scale = lax.rsqrt(jnp.mean(row * row, axis=-1, keepdims=True) + EPS)
+                normed[at * 2 + side, step : step + 32] = (row * scale * gains[0:1]).astype(low)
+        flat = normed[pl.ds(at * 2, 2)].reshape(pair_rows, width)
+        everything = dot(flat, heads_v[...].reshape(width, COLS))
+        raw = everything[:, 0:256]
+        projected[here] = raw
+        scale = lax.rsqrt(dot_fine(raw * raw, ones) * (1.0 / head) + EPS)
+        u = raw * scale * gains[2:3, 0:256]
+        cosine, sine = rotation(at)
+        turned = u * cosine + swapped(u) * sine
+        last = turned[:, 128:256]
+        queries[here, 0:128] = (turned[:, 0:128] * 0.125).astype(low)
+        queries[here, 128:256] = jnp.where(low_lanes, last * 0.125, 0.0).astype(low)
+        key = jnp.where(low_lanes, pltpu.roll(last, head, 1), 0.0)
+        value = jnp.where(low_lanes, everything[:, 256:COLS], 0.0)
+        both = (key, pltpu.roll(key, head, 1), value, pltpu.roll(value, head, 1))
+        for which, each in enumerate(both):
+            keys[which, here] = each.astype(low)
+        keys_t[0, :, here] = jnp.transpose(key).astype(low)
+        keys_t[1, :, here] = jnp.transpose(both[1]).astype(low)
+        values_t[0, :, here] = jnp.transpose(value).astype(low)
+        values_t[1, :, here] = jnp.transpose(both[3]).astype(low)
+
+    out.relay()
+    down.pair_done()
+    come(cotangent_move)
+    cotangent_spread.start()
+
+    def block(rank):
+        return pl.ds(pl.multiple_of(rank * tokens, tokens), tokens)
+
+    def both(ref, ranks, *lanes):
+        return jnp.concatenate([ref[(block(rank), *lanes)] for rank in ranks], axis=0)
+
+    def side_by_side(ref, row, ranks):
+        return jnp.concatenate([ref[row : row + 1, block(rank)] for rank in ranks], axis=1)
+
+    def half_of(number):
+        return slice(number * tokens, (number + 1) * tokens)
+
+    def core_at(at):
+        return (1 - place.core) * (1 - at) + place.core * at
+
+    chunk = 128
+    chunks = [slice(at, at + chunk) for at in range(0, span, chunk)]
+
+    def grown(here, queries_index):
+        keys_index = jnp.concatenate([index_column[here]] * 2, axis=1)
+        return jnp.where(keys_index <= queries_index, jnp.exp(scores[here]), 0.0)
+
+    def attend(ranks):
+        queries_index = side_by_side(index_row, 0, ranks)
+        sums = []
+        for number, (which, lanes) in enumerate(((0, 0), (1, 0), (0, 128))):
+            scores[...] = dot_turned(keys[which], both(queries, ranks, slice(lanes, lanes + 128)))
+            total = jnp.zeros((8, pair_rows), single)
+            for here in chunks:
+                weight = grown(here, queries_index)
+                probs[here] = weight.astype(low)
+                total = total + jnp.sum(weight.reshape(chunk // 8, 8, pair_rows), axis=0)
+            inverse = 1.0 / jnp.sum(total, axis=0, keepdims=True)
+            for side, rank in enumerate(ranks):
+                totals[number : number + 1, block(rank)] = inverse[:, half_of(side)]
+            sums.append(dot(values_t[which], probs[...]) * inverse)
+        first, last = sums[0] + sums[1], sums[2]
+        for side, rank in enumerate(ranks):
+            here = block(rank)
+            mixed_t[0:128, here] = first[:, half_of(side)].astype(low)
+            mixed_t[128:256, here] = last[:, half_of(side)].astype(low)
+            mixed[here, 0:128] = jnp.transpose(first[:, half_of(side)])
+            mixed[here, 128:256] = jnp.transpose(last[:, half_of(side)])
+
+    def in_turns(collect, make, before):
+        for turns in ((3, 1), (2, 0)):
+            before(turns)
+            for turn in turns:
+                make(place.ranks(turn)[1])
+                collect.send_near(turn)
+            for turn in turns:
+                make(place.ranks(turn)[0])
+            if turns[0] == 3:
+                collect.first_step()
+
+    def attend_to(turns):
+        chips = [place.chip_at(turn) for turn in turns]
+
+        @pl.loop(0, 2)
+        def _(at):
+            attend([core_at(at) * 4 + chip for chip in chips])
+
+        if turns[0] == 3:
+            cotangent_spread.relay(range(2))
+            gate_up.across(1)
+            hidden_spread.finish()
+            out.arrive()
+        else:
+            cotangent_spread.relay(range(2, PIECES))
+
+    def branch_part(rank):
+        here = block(rank)
+        weight = out_v[...].reshape(3 * 2 * rows_of, width)[0:256]
+        part[rank] = dot(mixed[here].astype(low), weight).astype(low)
+
+    in_turns(attention_collect, branch_part, attend_to)
+    cotangent_spread.relay_far()
+    attention_collect.second_step(row_sum)
+    gate_up.relay(0)
+    down.relay()
+
+    def second_norm(at, rows_here):
+        total = rows_own[rows_here].astype(single) + row_sum[rows_here]
+        middle[rows_here] = total
+        scale = lax.rsqrt(jnp.mean(total * total, axis=-1, keepdims=True) + EPS)
+        own_low[rows_here] = (total * scale * gains[1:2]).astype(low)
+        two_spread.start_piece(at)
+
+    attention_collect.third_step(row_sum, second_norm)
+    two_all[place.rank] = own_low[...]
+    attention_collect.finish()
+    cotangent_spread.arrive()
+    gate_up.arrive(0)
+    down.arrive()
+
+    def feed_forward(ranks, lanes, cut, joined, first_unit, count):
+        weight = gate_up_v[:, :, :, :, :, lanes].reshape(width, lanes.size)
+        normed_rows = jnp.concatenate([two_all[rank] for rank in ranks], axis=0)
+        gate_up_rows = dot(normed_rows, weight)
+        grad = jnp.concatenate([cotangent_all[rank] for rank in ranks], axis=0)
+        weight_down = down_v[...].reshape(units, width)[first_unit : first_unit + count]
+        grad_inner = dot_turned(grad, weight_down)
+        for side, rank in enumerate(ranks):
+            for step in range(0, tokens, 32):
+                here = slice(side * tokens + step, side * tokens + step + 32)
+                gate, up = cut(gate_up_rows[here])
+                back = grad_inner[here]
+                if gate.shape[1] > count:
+                    rest = jnp.zeros((32, gate.shape[1] - count), single)
+                    back = jnp.concatenate([back, rest], axis=1)
+                sigmoid = 1.0 / (1.0 + jnp.exp(-gate))
+                active = gate * sigmoid
+                inner[step : step + 32, 0 : gate.shape[1]] = active * up
+                grad_gate = back * up * sigmoid * (1.0 + gate * (1.0 - sigmoid))
+                rows_here = pl.ds(pl.multiple_of(rank * tokens + step, 32), 32)
+                unit_grad[rows_here, lanes] = joined(grad_gate, back * active).astype(low)
+            kept = pl.ds(first_unit, gate.shape[1])
+            inner_t[kept, block(rank)] = jnp.transpose(inner[:, 0 : gate.shape[1]]).astype(low)
+        return dot_turned(both(unit_grad, ranks, lanes), weight)
+
+    def feed_first(ranks):
+        back = feed_forward(
+            ranks,
+            unit_parts[0],
+            lambda values: (values[:, 0:early], values[:, early:]),
+            lambda gate, up: jnp.concatenate([gate, up], axis=1),
+            0,
+            early,
+        )
+        for side, rank in enumerate(ranks):
+            part[rank] = back[half_of(side)].astype(low)
+
+    def cut_second(values):
+        shared = values[:, late : late + 128]
+        return values[:, 0 : late + 128], jnp.concatenate(
+            [values[:, late + 128 :], pltpu.roll(shared, head, 1)], axis=1
+        )
+
+    def join_second(gate, up):
+        low_part = iota((gate.shape[0], 128), 1) < head
+        shared = jnp.where(low_part, gate[:, late:], pltpu.roll(up[:, late:], head, 1))
+        return jnp.concatenate([gate[:, 0:late], shared, up[:, 0:late]], axis=1)
+
+    def feed_second(ranks):
+        back = feed_forward(
+            ranks, unit_parts[1], cut_second, join_second, early, units - early
+        )
+        for side, rank in enumerate(ranks):
+            part[rank] = (part[rank].astype(single) + back[half_of(side)]).astype(low)
+
+    def units_weight_grad(lanes):
+        size = width // 4
+        for at in range(4):
+            columns = two_all[:, :, at * size : (at + 1) * size].reshape(span, size)
+            grad = dot_rows(columns, unit_grad[:, lanes]).astype(low)
+            chips = pl.ds(at % 2 * 2, 2)
+            gate_up_v[at // 2, chips, :, :, :, lanes] = grad.reshape(
+                (2,) + gate_up_v.shape[2:5] + (lanes.size,)
+            )
+
+    @pl.loop(0, RANKS // 2)
+    def _(at):
+        @pl.when(at == 0)
+        def _():
+            two_spread.arrive(["near"])
+
+        @pl.when(at == 1)
+        def _():
+            two_spread.relay(range(2, PIECES))
+            two_spread.arrive(["x_mate"])
+
+        @pl.when(at == 2)
+        def _():
+            two_spread.arrive(["z_mate"])
+
+        @pl.when(at == 3)
+        def _():
+            two_spread.arrive(["far_mate"])
+
+        feed_first(place.beside(at))
+
+        @pl.when(at == 0)
+        def _():
+            two_spread.relay(range(2))
+
+        @pl.when(at == 1)
+        def _():
+            two_spread.relay_far()
+            gate_up.relay(1)
+
+
+    gate_up.finish(0)
+    units_weight_grad(unit_parts[0])
+    gate_up_sums.start(0)
+    gate_up.arrive(1)
+
+    for turns in ((3, 1), (2, 0)):
+        chips = [place.chip_at(turn) for turn in turns]
+
+        @pl.loop(0, 2)
+        def _(at):
+            feed_second([core_at(at) * 4 + chip for chip in chips])
+
+            @pl.when(at == 0)
+            def _():
+                two_collect.begin(turns)
+
+        if turns[0] == 3:
+            two_collect.first_step()
+
+    gate_up_sums.across(0)
+    gate_up.finish(1)
+    down.finish()
+    units_weight_grad(unit_parts[1])
+    gate_up_sums.start(1)
+    two_collect.second_step(row_sum)
+    size = width // 3
+    for at in range(3):
+        lanes = slice(at * size, (at + 1) * size)
+        columns = cotangent_all[:, :, lanes].reshape(span, size)
+        grad = dot(inner_t[0:units], columns).astype(low)
+        down_grad[:, :, :, lanes] = grad.reshape(down_grad.shape[:3] + (size,))
+    down_sums.start()
+    gain_sums[...] = jnp.zeros(gain_sums.shape, single)
+    two_spread.finish()
+    cotangent_spread.finish()
+
+    def second_norm_back(at, rows_here):
+        mid = middle[rows_here]
+        scale = lax.rsqrt(jnp.mean(mid * mid, axis=-1, keepdims=True) + EPS)
+        grads = row_sum[rows_here]
+        gain_sums[1:2] += jnp.sum(grads * mid * scale, axis=0, keepdims=True)
+        own_grad = cotangent_all[place.rank, rows_here].astype(single)
+        total = own_grad + norm_back(mid, scale, grads * gains[1:2])
+        grad_middle[rows_here] = total
+        own_low[rows_here] = total.astype(low)
+        branch_spread.start_piece(at)
+
+    two_collect.third_step(row_sum, second_norm_back)
+    branch_all[place.rank] = own_low[...]
+    two_collect.finish()
+    key_grad[...] = jnp.zeros(key_grad.shape, single)
+    value_grad[...] = jnp.zeros(value_grad.shape, single)
+    pick = chosen(iota((8, 256), 1) // head == iota((8, 256), 0))
+
+    def attend_back(at, between):
+        ranks = place.beside(at)
+        weight = out_v[...].reshape(3 * 2 * rows_of, width)[0:256]
+        rows_here = jnp.concatenate([branch_all[rank] for rank in ranks], axis=0)
+        all_grad = dot_turned(rows_here, weight)
+        product = all_grad.astype(low).astype(single) * both(mixed, ranks, slice(0, 256))
+        inverse = jnp.concatenate([totals[:, block(rank)] for rank in ranks], axis=1)
+        all_delta = dot_fine_turned(pick, product) * inverse
+        high = inverse.astype(low)
+        rest = (inverse - high.astype(single)).astype(low)
+        all_grad = (all_grad * (dot_rows(high, pick) + dot_rows(rest, pick))).astype(low)
+        queries_index = side_by_side(index_row, 0, ranks)
+        turned = []
+        for number, (which, lanes) in enumerate(((0, 0), (1, 0), (0, 128))):
+            query = both(queries, ranks, slice(lanes, lanes + 128))
+            grad = all_grad[:, lanes : lanes + 128]
+            scores[...] = dot_turned(keys[which], query)
+            probs_grad[...] = dot_turned(keys[2 + which], grad)
+            for here in chunks:
+                weight = grown(here, queries_index)
+                probs[here] = weight.astype(low)
+                change = weight * (probs_grad[here] - all_delta[number : number + 1])
+                scores_grad[here] = change.astype(low)
+            value_grad[which] += dot(probs[...], grad)
+            key_grad[which] += dot(scores_grad[...], query)
+            turned.append(dot(keys_t[which], scores_grad[...]))
+            between(number)
+        first, last = turned[0] + turned[1], turned[2]
+        for side, rank in enumerate(ranks):
+            here = block(rank)
+            query_grad[here, 0:128] = jnp.transpose(first[:, half_of(side)]) * 0.125
+            query_grad[here, 128:256] = jnp.transpose(last[:, half_of(side)]) * 0.125
+
+    @pl.loop(0, 2)
+    def _(at):
+        @pl.when(at == 0)
+        def _():
+            branch_spread.arrive(["near"])
+
+        @pl.when(at == 1)
+        def _():
+            branch_spread.arrive(["x_mate"])
+
+        def between(number):
+            @pl.when(at == 0)
+            def _():
+                branch_spread.relay(((0, 1), (2,), (3,))[number])
+
+            if number == 0:
+                pl.when(at == 1)(branch_spread.relay_far)
+                pl.when(at == 1)(lambda: gate_up_sums.across(1))
+
+        attend_back(at, between)
+
+
+    @pl.loop(0, RANKS // 2)
+    def _(at):
+        here = pair(at)
+        rows_part = dot_rows(inner_t[0:units, here], down_v[...].reshape(units, width))
+        part[pl.ds(at * 2, 2)] = rows_part.astype(low).reshape(2, tokens, width)
+
+    down_collect.begin()
+    gate_up_sums.start_near()
+
+    @pl.loop(2, RANKS // 2)
+    def _(at):
+        @pl.when(at == 2)
+        def _():
+            branch_spread.arrive(["z_mate"])
+
+        @pl.when(at == 3)
+        def _():
+            branch_spread.arrive(["far_mate"])
+
+        def between(number):
+            if number == 0:
+                pl.when(at == 2)(down_collect.first_step)
+                pl.when(at == 3)(down_sums.across)
+
+        attend_back(at, between)
+
+    out.finish()
+    flat = branch_all[...].reshape(span, width)
+    out_v[0:2] = dot(mixed_t[0 : GROUP * head], flat).astype(low).reshape((2,) + out_v.shape[1:])
+    out_sums.start()
+
+    @pl.loop(0, RANKS // 2)
+    def _(at):
+        here = pair(at)
+        merged = []
+        for sums in (key_grad, value_grad):
+            total = jnp.where(low_lanes, sums[0, here] + pltpu.roll(sums[1, here], head, 1), 0.0)
+            merged.append(total)
+        second = query_grad[here, 128:256] + pltpu.roll(merged[0], head, 1)
+        grad = jnp.concatenate([query_grad[here, 0:128], second], axis=1)
+        cosine, sine = rotation(at)
+        turned = grad * cosine - swapped(grad) * sine
+        raw = projected[here]
+        scale = lax.rsqrt(dot_fine(raw * raw, ones) * (1.0 / head) + EPS)
+        gain_sums[2:3, 0:256] += jnp.sum(turned * raw * scale, axis=0, keepdims=True)
+        weighted = turned * gains[2:3, 0:256]
+        mean = dot_fine(weighted * raw, ones) * (1.0 / head)
+        back = scale * weighted - scale * scale * scale * raw * mean
+        heads_grad[here, 0:256] = back.astype(low)
+        heads_grad[here, 256:COLS] = merged[1].astype(low)
+
+    down_collect.second_step(row_sum)
+
+    def normed_part(rank):
+        here = block(rank)
+        part[rank] = dot_turned(heads_grad[here], heads_v[...].reshape(width, COLS)).astype(low)
+
+    branch_spread.finish()
+    down_collect.finish_near()
+    in_turns(last_collect, normed_part, lambda turns: None)
+    out_sums.across()
+    heads.finish()
+    size = width // 4
+    for at in range(4):
+        columns = normed[:, :, at * size : (at + 1) * size].reshape(span, size)
+        grad = dot_rows(columns, heads_grad[...]).astype(low)
+        chips = pl.ds(at % 2 * 2, 2)
+        heads_v[at // 2, chips] = grad.reshape((2,) + heads_v.shape[2:])
+    heads_sums.start()
+    heads_sums.start_near()
+    down_collect.third_step(row_sum)
+    block_low[...] = (middle[...] + row_sum[...]).astype(low)
+    go(block_move)
+    down_collect.finish()
+    last_collect.second_step(row_sum)
+    heads_sums.across()
+
+    def first_norm_back(at, rows_here):
+        values = rows_own[rows_here].astype(single)
+        scale = lax.rsqrt(jnp.mean(values * values, axis=-1, keepdims=True) + EPS)
+        grads = row_sum[rows_here]
+        gain_sums[0:1] += jnp.sum(grads * values * scale, axis=0, keepdims=True)
+        total = grad_middle[rows_here] + norm_back(values, scale, grads * gains[0:1])
+        in_low[rows_here] = total.astype(low)
+
+    last_collect.third_step(row_sum, first_norm_back)
+    go(in_move)
+    exchanges = []
+    for at, device in enumerate(
+        (place.mate, place.member(1, 0)[0], place.member(2, 0)[0], place.y_peer, place.z_peer)
+    ):
+        source = gain_sums if at == 0 else gain_parts.at[5 + at]
+        exchanges.append(links.link(source, gain_parts.at[at], device))
+
+    def exchange(at):
+        exchanges[at].wait_recv()
+        source = gain_sums if at == 0 else gain_parts.at[5 + at]
+        gain_parts[6 + at] = source[...] + gain_parts[at]
+        if at < 4:
+            exchanges[at + 1].start()
+
+    exchanges[0].start()
+    gate_up_sums.deal()
+    exchange(0)
+    down_sums.deal()
+    exchange(1)
+    out_sums.deal()
+    exchange(2)
+    heads_sums.deal()
+    exchange(3)
+    for each in (last_collect, down_sums, out_sums):
+        each.finish()
+    exchange(4)
+    total = gain_parts[10]
+    block_at = place.ctx * 4 + place.fsdp
+    pick_rows = chosen(iota((width, 128), 0) == iota((width, 128), 1) + block_at * rows_of)
+    in_block = iota((width, 128), 1) < rows_of
+    own = dot_fine(total, jnp.where(in_block, pick_rows, jnp.zeros_like(pick_rows)))
+    attn_gain_sum[...] = own[0:1, 0:rows_of]
+    ffn_gain_sum[...] = own[1:2, 0:rows_of]
+    lanes, columns = iota((256, 128), 0), iota((256, 128), 1)
+    gain_at = lanes % head + jnp.where(lanes >= GROUP * head, head, 0)
+    own = dot_fine(total[:, 0:256], chosen((gain_at == columns + block_at * 4) & (columns < 4)))
+    qk_gain_sum[...] = own[2:3, 0:4]
+    for copy in exchanges:
+        copy.wait_send()
+    gate_up_sums.finish()
+    low_part = iota((rows_of, 128), 1) < head
+
+    def joined_up(rank, parts):
+        first, second = (parts(rank + side) for side in range(2))
+        moved_by = pltpu.roll(second, head, 1)
+        count = first.shape[1] - 128
+        middle_tile = jnp.where(low_part, first[:, count:], moved_by[:, 0:128])
+        return jnp.concatenate([first[:, 0:count], middle_tile, moved_by[:, 128:]], axis=1)
+
+    def gate_part(rank):
+        return jnp.concatenate(
+            [
+                gate_up_sum[rank, :, 0:early],
+                gate_up_sum[rank, :, 2 * early : 2 * early + late + 128],
+            ],
+            axis=1,
+        ).astype(single)
+
+    def up_part(rank):
+        shared = gate_up_sum[rank, :, 2 * early + late : 2 * early + late + 128].astype(single)
+        return jnp.concatenate(
+            [
+                gate_up_sum[rank, :, early : 2 * early].astype(single),
+                gate_up_sum[rank, :, 2 * early + late + 128 :].astype(single),
+                pltpu.roll(shared, head, 1),
+            ],
+            axis=1,
+        )
+
+    for rank in range(0, RANKS, 2):
+        lanes = slice(rank * units, (rank + 2) * units)
+        gate_sum[:, lanes] = joined_up(rank, gate_part)
+        up_sum[:, lanes] = joined_up(rank, up_part)
+    heads_sums.finish()
+    for rank in range(0, RANKS, 2):
+        lanes = slice(rank * GROUP * head, (rank + 2) * GROUP * head)
+        query_sum[:, lanes] = joined_up(
+            rank, lambda at: heads_sum[at, :, 0:256].astype(single)
+        )
+        lanes = slice(rank * head, (rank + 2) * head)
+        first = heads_sum[rank, :, 128:256].astype(single)
+        second = heads_sum[rank + 1, :, 128:256].astype(single)
+        key_sum[:, lanes] = jnp.where(low_part, pltpu.roll(first, head, 1), second)
+        first = heads_sum[rank, :, 256:COLS].astype(single)
+        second = heads_sum[rank + 1, :, 256:COLS].astype(single)
+        value_sum[:, lanes] = jnp.where(low_part, first, pltpu.roll(second, head, 1))
+    come(block_move)
+    come(in_move)
+
+
+ANYWHERE = pl.BlockSpec(memory_space=pl.ANY)
+ON_CHIP = pl.BlockSpec(memory_space=pltpu.VMEM)
+
+
+def call(kernel, name, number, outs, scratch, ins, in_specs, out_specs):
+    return pl.pallas_call(
+        kernel,
+        out_shape=outs,
+        in_specs=in_specs,
+        out_specs=out_specs,
+        scratch_shapes=scratch,
+        name=name,
+        compiler_params=pltpu.CompilerParams(
+            collective_id=number, has_side_effects=True, vmem_limit_bytes=VMEM_BYTES
+        ),
+    )(*ins)
+
+
+def shape(dims, kind=jnp.bfloat16):
+    return jax.ShapeDtypeStruct(dims, kind)
+
+
+def copies(count):
+    return [pltpu.SemaphoreType.DMA((count,)), pltpu.SemaphoreType.DMA((count,))]
+def square_plan(
+    hidden_in,
+    cotangent,
+    block_order,
+    rotary_positions,
+    attn_gain,
+    qk_gain,
+    w_query,
+    key_projection,
+    value_projection,
+    w_output,
+    ffn_gain,
+    w_gate,
+    w_up,
+    w_down,
+):
+    single, low = jnp.float32, jnp.bfloat16
+    place = Place()
+    tokens, width = hidden_in.shape[1:]
+    span = RANKS * tokens
+    rows = w_query.shape[0]
+    ff = w_gate.shape[1] // RANKS
+    q_cols, head = GROUP * HEAD_SIZE, HEAD_SIZE
+    cols = 384
+    half_rows = tokens // 2
+    order = block_order[0]
+
+    early, cut = FIRST_UNITS, ff // 128 * 128
+    block, many = (tokens, width), (RANKS, tokens, width)
+
+    def held(*dims, kind=low):
+        return pltpu.VMEM(dims, kind)
+
+    results = call(
+        block_kernel,
+        "whole_block",
+        0,
+        [
+            shape(block),
+            shape(block),
+            shape(w_query.shape, single),
+            shape(key_projection.shape, single),
+            shape(value_projection.shape, single),
+            shape(w_gate.shape, single),
+            shape(w_up.shape, single),
+            shape(w_output.shape, single),
+            shape(w_down.shape, single),
+            shape((1, rows), single),
+            shape((1, rows), single),
+            shape((1, qk_gain.shape[0]), single),
+        ],
+        [
+            held(*many),
+            held(*many),
+            held(*many),
+            held(*many),
+            held(*many),
+            held(2, 4, 2, 2, rows, cols),
+            held(2, 4, 2, 2, rows, 2 * ff),
+            held(3, 2, *w_output.shape),
+            held(2, 2, *w_down.shape),
+            held(cut + 128, span),
+            held(span, 2 * ff),
+            held(span, 256, kind=single),
+            held(span, 256),
+            held(4, span, 128),
+            held(2, 128, span),
+            held(2, 128, span),
+            held(span, 256, kind=single),
+            held(256, span),
+            held(8, span, kind=single),
+            held(8, span, kind=single),
+            held(span, 128, kind=single),
+            held(160, 128, kind=single),
+            held(8, width, kind=single),
+            held(2, span, 128, kind=single),
+            held(2, span, 128, kind=single),
+            held(2, 2, *w_down.shape),
+            held(span, 256, kind=single),
+            held(span, 256, kind=single),
+            held(tokens, cut + 128 - early, kind=single),
+            held(8, width, kind=single),
+            held(11, 8, width, kind=single),
+            held(*block, kind=single),
+            held(*block, kind=single),
+            held(*block, kind=single),
+            held(*block),
+            held(*block),
+            held(*block),
+            held(*block),
+        ]
+        + collect_scratch(tokens, width)
+        + column_scratch((rows, 2 * ff))
+        + column_scratch((rows, cols))
+        + row_scratch(w_down.shape)
+        + row_scratch(w_output.shape)
+        + copies(4 + 10 + 13 + 6 + 4 * SPREAD_LINKS + 4 * COLLECT_LINKS + 22 + 6 + 5)
+        + [pltpu.SemaphoreType.DMA((11,))],
+        (
+            w_query, key_projection, value_projection, w_gate, w_up,
+            attn_gain[None], qk_gain[None], ffn_gain[None], block_order, rotary_positions,
+            w_output, w_down, hidden_in[0], cotangent[0],
+        ),
+        [ON_CHIP] * 10 + [ANYWHERE] * 4,
+        [ANYWHERE] * 2 + [ON_CHIP] * 10,
+    )
+    block_out, grad_in, query_sum, key_sum, value_sum, gate_sum, up_sum, out_sum, down_sum = results[:9]
+    attn_gain_sum, ffn_gain_sum, qk_gain_sum = results[9:]
+    return (
+        block_out[None],
+        grad_in[None],
+        attn_gain_sum[0],
+        qk_gain_sum[0],
+        query_sum,
+        key_sum,
+        value_sum,
+        out_sum,
+        ffn_gain_sum[0],
+        gate_sum,
+        up_sum,
+        down_sum,
+    )
+
+
 def solution(mesh):
+    square = dict(mesh.shape) == {"ctx": 8, "fsdp": 4}
+    plan = square_plan if square else general_plan
     return jax.shard_map(
-        on_device,
+        plan,
         mesh=mesh,
         in_specs=(
             P("fsdp", "ctx", None),

time: 2410 us -> 294 us (0.12)
  waiting for transfers between devices: 1080 us -> 0 us
  local copies, waits for them, and re-layouts: 612 us -> 10.7 us
  other arithmetic: 443 us -> 0 us
  Pallas kernels: 0 us -> 279 us
  matrix products: 137 us -> 0 us
  starting transfers between devices: 49.7 us -> 0 us
  blocking collectives: 40.7 us -> 0 us
    all_gather x9 -> x0, waiting for transfers between devices: 508 us -> none  [the longest x1 101 us: on_device(): lax.all_gather(w_gate, ('ctx', 'fsdp'), axis=0, tiled=True)]
    all_to_all x10 -> x0, waiting for transfers between devices: 469 us -> none  [the longest x1 170 us: on_device(): lax.all_to_all(grad_w_gate[None].astype(jnp.bfloat16), ('ctx', 'fsdp'), s...]
    unnamed x8 -> x0, other arithmetic: 358 us -> none
    unnamed x147 -> x34, local copies, waits for them, and re-layouts: 350 us -> 10.7 us
    pallas_call x0 -> x1, Pallas kernels: none -> 279 us  [call(): pl.pallas_call(kernel, out_shape=outs, in_specs=in_specs, out_specs=out_s...]
    convert_element_type x11 -> x0, local copies, waits for them, and re-layouts: 211 us -> none  [the longest x1 52.2 us: on_device(): grad_w_output[None].astype(jnp.bfloat16)]
    dot_general x35 -> x0, matrix products: 137 us -> none  [the longest x1 13.1 us: on_device(): jnp.einsum('td,fd->tf', grad_out, down_w, preferred_element_type=single_f...]
    unnamed x13 -> x0, waiting for transfers between devices: 107 us -> none
  transfers between devices with their start and end apart: 21 -> 0, of which waited for: 16 -> 0; matrix products, arithmetic and copies ran while one was open for 42% -> 0% of each run, Pallas kernels for 0% -> 0%
where the time goes in v1:
time: 294 us; the launch traced here: 291 us
  Pallas kernels  279 us (95%)
  local copies, waits for them, and re-layouts  10.7 us (4%)
    pallas_call x1, Pallas kernels, call(): pl.pallas_call(kernel, out_shape=outs, in_specs=in_specs, out_specs=out_s...  279 us
    unnamed x34, local copies, waits for them, and re-layouts  10.7 us

profile of v1, /device:TPU:6, one launch (start us, length us, event | category | flops | bytes accessed | tf_op | source)
XLA Modules:
  0.0 290.7 jit_solution(7188708425756061616)
XLA Ops:
  0.6 279.3 %whole_block.1 = (bf16[128,1536]{1,0:T(8,128)(2,1)}, bf16[128,1536]{1,0:T(8,128)(2,1)}, f32[48,1536]{1,0:T(8,128)}, f32[48,512]{1,0:T(8,128)}, f32[48,512]{1,0:T...) custom-call(bf16[48,1536]{1,0:T(8,128)(2,1)} %query_w.1, ...), custom_call_target="tpu_custom_call" | custom-call | tf_op jit(solution)/shard_map/whole_block/pallas_call | solution.py:1696
  279.9 0.0 copy-start.3
  280.0 0.0 copy-start.10
  280.0 1.8 copy.38
  281.8 0.0 copy-done.3
  281.8 0.0 copy-start.9
  281.8 0.0 copy-start.5
  281.8 0.0 copy-start.7
  281.8 0.0 copy-start.6
  281.8 0.0 copy-start.4
  281.8 0.7 copy.39
  282.6 0.0 copy-done.10
  282.6 0.0 copy-start.2
  282.6 0.5 copy.40
  283.1 0.0 copy-done.9
  283.1 0.5 copy.41
  283.6 0.0 copy-done.5
  283.6 0.7 copy.42
  284.3 0.0 copy-done.7
  284.3 0.6 copy.43
  284.9 0.0 copy-done.6
  285.0 0.6 copy.44
  285.6 0.0 copy-done.4
  285.6 0.0 copy-start.8
  285.6 0.7 copy.45
  286.3 0.0 copy-done.8
  286.3 0.5 copy.46
  286.8 0.0 copy-done.2
  286.8 0.0 copy-start.1
  286.8 0.9 copy.47
  287.7 0.6 copy-done.1
  288.3 0.0 copy-start
  288.3 0.9 copy.48
  289.2 0.6 copy-done
  289.8 0.9 copy.49
Async XLA Ops:
  279.9 1.8 copy-start.3
  280.0 2.6 copy-start.10
  281.8 1.3 copy-start.9
  281.8 1.8 copy-start.5
  281.8 2.5 copy-start.7
  281.8 3.2 %copy-start.6 = (f32[48,512]{1,0:T(8,128)S(1)}, f32[48,512]{1,0:T(8,128)}, u32[]{:S(2)}) copy-start(f32[48,512]{1,0:T(8,128)} %get-tuple-element.54) | copy-start | bytes 294916
  281.8 3.8 %copy-start.4 = (f32[48,1536]{1,0:T(8,128)S(1)}, f32[48,1536]{1,0:T(8,128)}, u32[]{:S(2)}) copy-start(f32[48,1536]{1,0:T(8,128)} %get-tuple-element.55) | copy-start | bytes 884740
  282.6 4.3 %copy-start.2 = (f32[48,4608]{1,0:T(8,128)S(1)}, f32[48,4608]{1,0:T(8,128)}, u32[]{:S(2)}) copy-start(f32[48,4608]{1,0:T(8,128)} %get-tuple-element.57) | copy-start | bytes 2654212
  285.6 0.7 copy-start.8
  286.8 1.5 copy-start.1
  288.3 1.5 copy-start
